TPU v7x, 128 devices: a whole 4x4x4 slice. The times are simulated.
128 devices in a mesh: ctx: 16 (over y, z), fsdp: 8 (over x, core).
Axes of the slice: x: 4, y: 4, z: 4, core: 2. Of those that a mesh axis runs over, the one named last changes fastest.
Arguments:
- tokens: bfloat16 [8, 2048, 1088], P('fsdp', 'ctx'), may hold values from -6 to 6
- grad_out: bfloat16 [8, 2048, 1088], P('fsdp', 'ctx'), may hold values from -6 to 6
- group_table: int32 [32], replicated, may hold values from 0 to 31, as said below
- doc_ids: int32 [8, 2048], P('fsdp'), may hold values from 0 to 2, as said below
- norm_gains: bfloat16 [2, 1088], P(None, 'fsdp'), may hold values from 0.5 to 1.5
- norm_biases: bfloat16 [2, 1088], P(None, 'fsdp'), may hold values from -1.796875 to 1.796875
- w_qkv: bfloat16 [1088, 3264], P('fsdp'), may hold values from -0.1875 to 0.1875
- qv_bias: bfloat16 [2, 1088], P(None, 'fsdp'), may hold values from -3 to 3
- w_out: bfloat16 [1088, 1088], P('fsdp'), may hold values from -3 to 3
- out_biases: bfloat16 [2, 1088], P(None, 'fsdp'), may hold values from -1.796875 to 1.796875
- w_up: bfloat16 [1088, 4352], P('fsdp'), may hold values from -0.1875 to 0.1875
- up_bias: bfloat16 [4352], P('fsdp'), may hold values from -1.796875 to 1.796875
- w_down: bfloat16 [4352, 1088], P('fsdp'), may hold values from -0.09375 to 0.09375
Outputs:
- block_out: bfloat16 [8, 2048, 1088], P('fsdp', 'ctx')
- grad_tokens: bfloat16 [8, 2048, 1088], P('fsdp', 'ctx')
- grad_norm_gains: float32 [2, 1088], P(None, 'fsdp')
- grad_norm_biases: float32 [2, 1088], P(None, 'fsdp')
- grad_w_qkv: float32 [1088, 3264], P('fsdp')
- grad_qv_bias: float32 [2, 1088], P(None, 'fsdp')
- grad_w_out: float32 [1088, 1088], P('fsdp')
- grad_out_biases: float32 [2, 1088], P(None, 'fsdp')
- grad_w_up: float32 [1088, 4352], P('fsdp')
- grad_up_bias: float32 [4352], P('fsdp')
- grad_w_down: float32 [4352, 1088], P('fsdp')
Inputs may be any that keep to these rules, and one draw needn't show every extreme that they name: `group_table`: entries 2i and 2i+1 sum to 31 and all entries differ. `doc_ids`: along increasing positions of a sequence the ids never fall; id 0 holds at least the first half of the positions.
All inputs are finite; a program needn't handle non-finite values.
Results may differ from a plain program's by a relative error of at most 0.025.
Values may be sent and summed in bfloat16 or wider, within the bound.
No kernel may reach another device: no remote copies, remote signals or barrier semaphores. Data moves between devices by JAX's collectives and lax.ppermute only.
A program may use at most 256 MiB of HBM per device.

v0:
```python
from functools import partial

import jax
import jax.numpy as jnp
from jax import lax
from jax.sharding import PartitionSpec as P

HEADS = 17
HD = 64


epsilon = 1e-05
masked_value = -1e30


def side_by_side(arrays, axis, dim, along):
    both = jnp.concatenate(arrays, axis=along)
    out, at, done = (lax.all_gather(both, axis, axis=dim, tiled=True), 0, [])
    for a in arrays:
        done.append(lax.slice_in_dim(out, at, at + a.shape[along], axis=along))
        at += a.shape[along]
    return tuple(done)


def side_by_side_2(arrays, axis, dim, along):
    ends, at = ([], 0)
    for a in arrays[:-1]:
        at += a.shape[along]
        ends.append(at)
    both = jnp.concatenate(arrays, axis=along)
    return tuple(
        jnp.split(lax.psum_scatter(both, axis, scatter_dimension=dim, tiled=True), ends, axis=along)
    )


def cut_along(x, dim, peers):
    before, after = (x.shape[:dim], x.shape[dim + 1 :])
    return jnp.moveaxis(x.reshape(*before, peers, -1, *after), dim, 0)


def sent_and_summed(x, axis, dim):
    peers = lax.axis_size(axis)
    pieces = lax.all_to_all(cut_along(x, dim, peers), axis, 0, 0, tiled=True)
    return jnp.sum(pieces.astype(jnp.float32), axis=0)


def sent_together(arrays, axis, dim, along):
    ends, at = ([], 0)
    for a in arrays[:-1]:
        at += a.shape[along]
        ends.append(at)
    both = jnp.concatenate(arrays, axis=along)
    return tuple(jnp.split(sent_and_summed(both, axis, dim), ends, axis=along))


def contract_rows(left_rows, right_rows):
    return lax.dot_general(
        left_rows, right_rows, (((0,), (0,)), ((), ())), preferred_element_type=jnp.float32
    )


def contract_cols(left_rows, right_rows):
    return lax.dot_general(
        left_rows, right_rows, (((1,), (1,)), ((), ())), preferred_element_type=jnp.float32
    )


def norm_forward(values, gain_row, shifts):
    row_mean = jnp.mean(values, axis=-1, keepdims=True)
    centred = values - row_mean
    variance = jnp.mean(centred * centred, axis=-1, keepdims=True)
    inverse = lax.rsqrt(variance + epsilon)
    scaled = centred * inverse
    return (scaled * gain_row + shifts, scaled, inverse)


def norm_backward(grad_norm, scaled, inverse, gain_row):
    grad_scaled = grad_norm * gain_row
    return inverse * (
        grad_scaled
        - jnp.mean(grad_scaled, axis=-1, keepdims=True)
        - scaled * jnp.mean(grad_scaled * scaled, axis=-1, keepdims=True)
    )


def row_term(left_rows, right_rows):
    return contract_rows(left_rows, right_rows)


def per_device(
    tokens,
    grad_out,
    group_table,
    doc_ids,
    norm_gains,
    norm_biases,
    w_qkv,
    qv_bias,
    w_out,
    out_biases,
    w_up,
    up_bias,
    w_down,
):
    shards = (w_qkv, w_out, w_up, w_down, norm_gains, norm_biases, qv_bias, out_biases, up_bias)
    gathered = (
        *side_by_side((shards[0], shards[1], shards[2]), "fsdp", 0, 1),
        lax.all_gather(shards[3], "fsdp", axis=0, tiled=True),
        *side_by_side((shards[4], shards[5], shards[6], shards[7]), "fsdp", 1, 0),
        lax.all_gather(shards[8], "fsdp", axis=0, tiled=True),
    )
    full_qkv, full_out, full_up, full_down = (gathered[0], gathered[1], gathered[2], gathered[3])
    gains_float = gathered[4].astype(jnp.float32)
    shifts_float = gathered[5].astype(jnp.float32)
    qv_float = gathered[6].astype(jnp.float32)
    outb_float = gathered[7].astype(jnp.float32)
    upb_float = gathered[8].astype(jnp.float32)
    seq_count, own_rows, model_width = tokens.shape
    seq_len = doc_ids.shape[1]
    ctx_count = lax.axis_size("ctx")
    group_rows = seq_len // (2 * ctx_count)
    row_index = jnp.arange(seq_len, dtype=jnp.int32)
    key_pos = jnp.take(group_table, row_index // group_rows) * group_rows + row_index % group_rows
    first_row = lax.axis_index("ctx") * own_rows
    query_pos = lax.dynamic_slice_in_dim(key_pos, first_row, own_rows)
    query_doc = lax.dynamic_slice_in_dim(doc_ids, first_row, own_rows, axis=1)
    attn_scale = HD ** (-0.5)

    def masked_scores(query_rows, keys_rows, query_docs, key_docs):
        query_heads = query_rows.reshape(query_rows.shape[0], HEADS, HD)
        key_heads = keys_rows.reshape(keys_rows.shape[0], HEADS, HD)
        raw_scores = jnp.einsum(
            "qhd,khd->hqk", query_heads, key_heads, preferred_element_type=jnp.float32
        )
        allowed = (key_pos[None, :] <= query_pos[:, None]) & (
            key_docs[None, :] == query_docs[:, None]
        )
        return jnp.where(allowed[None], raw_scores * attn_scale, masked_value)

    def attend_forward(member):
        query_rows, keys_rows, values_rows, query_docs, key_docs = member
        scores = masked_scores(query_rows, keys_rows, query_docs, key_docs)
        row_top = jnp.max(scores, axis=-1, keepdims=True)
        exponent = jnp.exp(scores - row_top)
        row_total = jnp.sum(exponent, axis=-1, keepdims=True)
        attn_probs = (exponent / row_total).astype(jnp.bfloat16)
        mixed_heads = jnp.einsum(
            "hqk,khd->qhd",
            attn_probs,
            values_rows.reshape(-1, HEADS, HD),
            preferred_element_type=jnp.float32,
        )
        return (
            mixed_heads.reshape(query_rows.shape[0], -1).astype(jnp.bfloat16),
            row_top + jnp.log(row_total),
        )

    def attend_backward(member):
        query_rows, keys_rows, values_rows, grad_rows, log_total, query_docs, key_docs = member
        scores = masked_scores(query_rows, keys_rows, query_docs, key_docs)
        attn_probs = jnp.exp(scores - log_total)
        grad_heads = grad_rows.reshape(-1, HEADS, HD)
        grad_probs = jnp.einsum(
            "qhd,khd->hqk",
            grad_heads,
            values_rows.reshape(-1, HEADS, HD),
            preferred_element_type=jnp.float32,
        )
        delta_rows = jnp.sum(attn_probs * grad_probs, axis=-1, keepdims=True)
        grad_scores = (attn_probs * (grad_probs - delta_rows) * attn_scale).astype(jnp.bfloat16)
        grad_query = jnp.einsum(
            "hqk,khd->qhd",
            grad_scores,
            keys_rows.reshape(-1, HEADS, HD),
            preferred_element_type=jnp.float32,
        )
        grad_key = jnp.einsum(
            "hqk,qhd->khd",
            grad_scores,
            query_rows.reshape(-1, HEADS, HD),
            preferred_element_type=jnp.float32,
        )
        grad_value = jnp.einsum(
            "hqk,qhd->khd",
            attn_probs.astype(jnp.bfloat16),
            grad_heads,
            preferred_element_type=jnp.float32,
        )
        return (
            grad_query.reshape(query_rows.shape[0], -1).astype(jnp.bfloat16),
            grad_key.reshape(keys_rows.shape[0], -1),
            grad_value.reshape(keys_rows.shape[0], -1),
        )

    flat_tokens = tokens.reshape(-1, model_width).astype(jnp.float32)
    normed, scaled_one, inverse_one = norm_forward(flat_tokens, gains_float[0], shifts_float[0])
    normed_low = normed.astype(jnp.bfloat16)
    projected = jnp.dot(normed_low, full_qkv, preferred_element_type=jnp.float32)
    queries = (projected[:, :model_width] + qv_float[0]).astype(jnp.bfloat16)
    keys_own = projected[:, model_width : 2 * model_width].astype(jnp.bfloat16)
    values_own = (projected[:, 2 * model_width :] + qv_float[1]).astype(jnp.bfloat16)
    keys_all, values_all = side_by_side(
        (
            keys_own.reshape(seq_count, own_rows, model_width),
            values_own.reshape(seq_count, own_rows, model_width),
        ),
        "ctx",
        1,
        0,
    )
    query_seq = queries.reshape(seq_count, own_rows, model_width)
    mixed_seq, log_total = lax.map(
        attend_forward, (query_seq, keys_all, values_all, query_doc, doc_ids)
    )
    mixed_flat = mixed_seq.reshape(-1, model_width)
    attended = jnp.dot(mixed_flat, full_out, preferred_element_type=jnp.float32) + outb_float[0]
    residual = flat_tokens + attended
    normed_two, scaled_two, inverse_two = norm_forward(residual, gains_float[1], shifts_float[1])
    normed_two_low = normed_two.astype(jnp.bfloat16)
    hidden_pre = jnp.dot(normed_two_low, full_up, preferred_element_type=jnp.float32) + upb_float
    hidden_act = jax.nn.gelu(hidden_pre, approximate=True).astype(jnp.bfloat16)
    block_out = (
        (
            residual
            + jnp.dot(hidden_act, full_down, preferred_element_type=jnp.float32)
            + outb_float[1]
        )
        .astype(jnp.bfloat16)
        .reshape(tokens.shape)
    )
    regathered = (
        *side_by_side((shards[0], shards[1], shards[2]), "fsdp", 0, 1),
        lax.all_gather(shards[3], "fsdp", axis=0, tiled=True),
        *side_by_side((shards[4], shards[5], shards[6], shards[7]), "fsdp", 1, 0),
        lax.all_gather(shards[8], "fsdp", axis=0, tiled=True),
    )
    back_qkv, back_out, back_up, back_down = (
        regathered[0],
        regathered[1],
        regathered[2],
        regathered[3],
    )
    back_gains = regathered[4].astype(jnp.float32)
    grad_flat = grad_out.reshape(-1, model_width)
    grad_float = grad_flat.astype(jnp.float32)
    grad_hidden = contract_cols(grad_flat, back_down)
    unused_value, gelu_pull = jax.vjp(partial(jax.nn.gelu, approximate=True), hidden_pre)
    grad_pre = gelu_pull(grad_hidden)[0].astype(jnp.bfloat16)
    grad_norm_two = contract_cols(grad_pre, back_up)
    grad_residual = grad_float + norm_backward(
        grad_norm_two, scaled_two, inverse_two, back_gains[1]
    )
    grad_attended = grad_residual.astype(jnp.bfloat16)
    grad_mixed = contract_cols(grad_attended, back_out).astype(jnp.bfloat16)
    grad_query, key_terms, value_terms = lax.map(
        attend_backward,
        (
            query_seq,
            keys_all,
            values_all,
            grad_mixed.reshape(seq_count, own_rows, model_width),
            log_total,
            query_doc,
            doc_ids,
        ),
    )
    grad_keys, grad_values = tuple(
        (
            part.astype(jnp.float32)
            for part in side_by_side_2(
                (key_terms.astype(jnp.bfloat16), value_terms.astype(jnp.bfloat16)), "ctx", 1, 0
            )
        )
    )
    grad_query_flat = grad_query.reshape(-1, model_width)
    grad_keys_low = grad_keys.reshape(-1, model_width).astype(jnp.bfloat16)
    grad_values_low = grad_values.reshape(-1, model_width).astype(jnp.bfloat16)
    grad_qkv = jnp.concatenate([grad_query_flat, grad_keys_low, grad_values_low], axis=1)
    grad_normed = contract_cols(grad_qkv, back_qkv)
    grad_tokens = (
        (grad_residual + norm_backward(grad_normed, scaled_one, inverse_one, back_gains[0]))
        .astype(jnp.bfloat16)
        .reshape(tokens.shape)
    )
    gain_terms = jnp.stack(
        [jnp.sum(grad_normed * scaled_one, axis=0), jnp.sum(grad_norm_two * scaled_two, axis=0)]
    )
    shift_terms = jnp.stack([jnp.sum(grad_normed, axis=0), jnp.sum(grad_norm_two, axis=0)])
    qv_terms = jnp.stack(
        [
            jnp.sum(grad_query_flat.astype(jnp.float32), axis=0),
            jnp.sum(grad_values_low.astype(jnp.float32), axis=0),
        ]
    )
    outb_terms = jnp.stack(
        [jnp.sum(grad_attended.astype(jnp.float32), axis=0), jnp.sum(grad_float, axis=0)]
    )
    upb_terms = jnp.sum(grad_pre.astype(jnp.float32), axis=0)
    small_sums = (
        *sent_together(
            (
                gain_terms.astype(jnp.bfloat16),
                shift_terms.astype(jnp.bfloat16),
                qv_terms.astype(jnp.bfloat16),
                outb_terms.astype(jnp.bfloat16),
            ),
            "fsdp",
            1,
            0,
        ),
        sent_and_summed(upb_terms.astype(jnp.bfloat16), "fsdp", 0),
    )
    qkv_shard = lax.psum_scatter(
        row_term(normed_low, grad_qkv).astype(jnp.bfloat16), "fsdp", scatter_dimension=0, tiled=True
    )
    out_shard = lax.psum_scatter(
        row_term(mixed_flat, grad_attended).astype(jnp.bfloat16),
        "fsdp",
        scatter_dimension=0,
        tiled=True,
    )
    up_shard = lax.psum_scatter(
        row_term(normed_two_low, grad_pre).astype(jnp.bfloat16),
        "fsdp",
        scatter_dimension=0,
        tiled=True,
    )
    down_shard = lax.psum_scatter(
        row_term(hidden_act, grad_flat).astype(jnp.bfloat16),
        "fsdp",
        scatter_dimension=0,
        tiled=True,
    )
    summed = (
        lax.psum(small_sums[0].astype(jnp.bfloat16), "ctx").astype(jnp.float32),
        lax.psum(small_sums[1].astype(jnp.bfloat16), "ctx").astype(jnp.float32),
        lax.psum(qkv_shard, "ctx").astype(jnp.float32),
        lax.psum(small_sums[2].astype(jnp.bfloat16), "ctx").astype(jnp.float32),
        lax.psum(out_shard, "ctx").astype(jnp.float32),
        lax.psum(small_sums[3].astype(jnp.bfloat16), "ctx").astype(jnp.float32),
        lax.psum(up_shard, "ctx").astype(jnp.float32),
        lax.psum(small_sums[4].astype(jnp.bfloat16), "ctx").astype(jnp.float32),
        lax.psum(down_shard, "ctx").astype(jnp.float32),
    )
    return (
        block_out,
        grad_tokens,
        summed[0],
        summed[1],
        summed[2],
        summed[3],
        summed[4],
        summed[5],
        summed[6],
        summed[7],
        summed[8],
    )


def solution(mesh):
    return jax.shard_map(
        per_device,
        mesh=mesh,
        in_specs=(
            P("fsdp", "ctx", None),
            P("fsdp", "ctx", None),
            P(),
            P("fsdp", None),
            P(None, "fsdp"),
            P(None, "fsdp"),
            P("fsdp", None),
            P(None, "fsdp"),
            P("fsdp", None),
            P(None, "fsdp"),
            P("fsdp", None),
            P("fsdp"),
            P("fsdp", None),
        ),
        out_specs=(
            P("fsdp", "ctx", None),
            P("fsdp", "ctx", None),
            P(None, "fsdp"),
            P(None, "fsdp"),
            P("fsdp", None),
            P(None, "fsdp"),
            P("fsdp", None),
            P(None, "fsdp"),
            P("fsdp", None),
            P("fsdp"),
            P("fsdp", None),
        ),
        check_vma=False,
    )
```

profile of v0, /device:TPU:0, one launch (start us, length us, event | category | flops | bytes accessed | tf_op | source)
XLA Modules:
  0.0 797.7 jit_solution(2454151212390462647)
XLA Ops:
  13.3 13.3 %all-gather = bf16[8,136,8]{1,2,0:T(8,128)(2,1)S(1)} all-gather(bf16[1,136,8]{1,2,0:T(8,128)(2,1)S(1)} %maximum_bitcast_fusion), channel_id=1, replica_groups=mesh['ctx'=16,'fsdp'=8] {'fsdp'}, dimensions={0}, use_global_device_ids=true | all-gather | bytes 19584 | tf_op jit(solution)/shard_map/all_gather | solution.py:18
  27.7 81.4 %all-gather.5.cloned.1.call-done = bf16[1088,8704]{1,0:T(8,128)(2,1)} async-done(((bf16[136,8704]{1,0:T(8,128)(2,1)}), bf16[1088,8704]{1,0:T(8,128)(2,1)}) %all-gather.5.cloned.1.call-update) | async-done | bytes 18939920 | tf_op jit(solution)/shard_map/all_gather | solution.py:18
  119.1 25.4 %all-reduce = bf16[4352]{0:T(1024)(128)(2,1)S(1)} all-reduce(bf16[4352]{0:T(1024)(128)(2,1)S(1)} %dynamic-update-slice), channel_id=1, replica_groups=mesh['ctx'=16,'fsdp'=8] {'fsdp'}, use_global_device_ids=true, to_apply=%add | all-reduce | flops 4352 | bytes 17408
  151.5 15.8 %fusion.102 = s32[2048]{0:T(1024)S(1)} fusion(pred[2048]{0:T(1024)(128)(4,1)S(1)} %compare_reduce_fusion, pred[2048]{0:T(1024)(128)(4,1)S(1)} %compare_reduce_fusion.1, pred[2048]{0:T(1024)(128)(4,1)S(1)} %compare_reduce_fusion.2, pred[2048]{0:T(1024)(128)(4,1)S(1)} %compare_reduce_fusion.3, pred[2048]{0:T(1024)(128)(4,1)S(1)} %compare_reduce_fusion.4, ...), kind=kLoop, calls=%fused_computation.160 | loop fusion | flops 94208 | bytes 67684 | tf_op jit(solution)/shard_map/add | solution.py:123
  167.7 31.1 %all-gather.7.cloned.1.call-done = bf16[2,2048,1088]{1,2,0:T(8,128)(2,1)} async-done(((bf16[2,128,1088]{1,2,0:T(8,128)(2,1)}), bf16[2,2048,1088]{1,2,0:T(8,128)(2,1)}) %all-gather.7.cloned.1.call-update) | async-done | bytes 8912912 | tf_op jit(solution)/shard_map/all_gather | solution.py:18
  205.9 9.0 %fusion.3 = (f32[17,128]{1,0:T(8,128)S(1)}, f32[17,128,2048]{2,1,0:T(8,128)}) fusion(pred[128,2048]{1,0:T(8,128)(4,1)S(1)} %compare_and_fusion, bf16[128,17,64]{0,2,1:T(8,128)(2,1)S(1)} %bitcast.150, bf16[2048,17,64]{0,2,1:T(8,128)(2,1)S(1)} %bitcast.141), kind=kOutput, calls=%fused_computation.12 | convolution fusion | flops 583792512 | bytes 22831616 | tf_op jit(solution)/shard_map/while/body/eval_jaxpr/qhd,khd->hqk/dot_general | solution.py:132
  214.9 10.5 %fusion.2 = f32[17,128]{1,0:T(8,128)S(1)} fusion(f32[17,128,2048]{2,1,0:T(8,128)} %get-tuple-element.155, f32[17,128]{1,0:T(8,128)S(1)} %get-tuple-element.154, pred[128,2048]{1,0:T(8,128)(4,1)S(1)} %compare_and_fusion), kind=kLoop, calls=%fused_computation.10 | loop fusion | flops 17823616 | bytes 18105344 | tf_op jit(solution)/shard_map/while/body/eval_jaxpr/reduce_sum | solution.py:145
  225.4 12.8 %fusion.66 = bf16[17,64,128]{2,1,0:T(8,128)(2,1)S(1)} fusion(bf16[2048,17,64]{0,2,1:T(8,128)(2,1)} %bitcast.143, f32[17,128,2048]{2,1,0:T(8,128)} %get-tuple-element.155, f32[17,128]{1,0:T(8,128)S(1)} %fusion.2, f32[17,128]{1,0:T(8,128)S(1)} %get-tuple-element.154, pred[128,2048]{1,0:T(8,128)(4,1)S(1)} %compare_and_fusion), kind=kOutput, calls=%fused_computation.62 | convolution fusion | flops 592846848 | bytes 22840320 | tf_op jit(solution)/shard_map/while/body/eval_jaxpr/hqk,khd->qhd/dot_general | solution.py:147
  248.8 7.7 all-gather.9.cloned.1.call-done
  274.6 8.6 %fusion.137 = f32[17,128,2048]{2,1,0:T(8,128)} fusion(bf16[128,17,64]{0,2,1:T(8,128)(2,1)S(1)} %bitcast.156, bf16[2048,17,64]{0,2,1:T(8,128)(2,1)S(1)} %bitcast.146), kind=kOutput, calls=%fused_computation.212 | convolution fusion | flops 570425344 | bytes 22560768 | tf_op jit(solution)/shard_map/while/body/eval_jaxpr/qhd,khd->hqk/dot_general | solution.py:163
  283.2 13.2 %fusion.47 = bf16[17,64,2048]{2,1,0:T(8,128)(2,1)} fusion(bf16[128,17,64]{0,2,1:T(8,128)(2,1)S(1)} %bitcast.157, f32[17,128,2048]{2,1,0:T(8,128)} %get-tuple-element.155, f32[17,128]{1,0:T(8,128)S(1)} %log_add_fusion, pred[128,2048]{1,0:T(8,128)(4,1)S(1)} %compare_and_fusion), kind=kOutput, calls=%fused_computation.41 | convolution fusion | flops 590479360 | bytes 22831616 | tf_op jit(solution)/shard_map/while/body/eval_jaxpr/hqk,qhd->khd/dot_general | solution.py:183
  296.4 35.3 %fusion.50 = bf16[17,64,2048]{2,1,0:T(8,128)(2,1)} fusion(bf16[128,17,64]{0,2,1:T(8,128)(2,1)} %bitcast.151, f32[17,128,2048]{2,1,0:T(8,128)} %fusion.137, f32[17,128,2048]{2,1,0:T(8,128)} %get-tuple-element.155, f32[17,128]{1,0:T(8,128)S(1)} %log_add_fusion, pred[128,2048]{1,0:T(8,128)(4,1)S(1)} %compare_and_fusion), kind=kOutput, calls=%fused_computation.42 | convolution fusion | flops 621678720 | bytes 40657408 | tf_op jit(solution)/shard_map/while/body/eval_jaxpr/hqk,qhd->khd/dot_general | solution.py:177
  331.7 8.0 pad_maximum_fusion
  339.7 23.8 %copy.30 = bf16[2,2048,1088]{2,0,1:T(2,128)(2,1)} copy(bf16[2,2048,1088]{1,2,0:T(8,128)(2,1)} %pad_maximum_fusion) | data formatting | bytes 17825792
  363.5 19.1 %reshape.477 = bf16[2048,2176]{1,0:T(8,128)(2,1)} reshape(bf16[2048,2,1088]{2,1,0:T(2,128)(2,1)} %bitcast.140) | data formatting | bytes 17825792
  399.8 34.6 %fusion.133 = (bf16[17,64]{1,0:T(8,128)(2,1)S(1)}, bf16[17,64,128]{2,1,0:T(8,128)(2,1)}) fusion(bf16[2048,17,64]{0,2,1:T(8,128)(2,1)} %bitcast.142, f32[17,128,2048]{2,1,0:T(8,128)} %fusion.137, f32[17,128,2048]{2,1,0:T(8,128)} %get-tuple-element.155, f32[17,128]{1,0:T(8,128)S(1)} %log_add_fusion, pred[128,2048]{1,0:T(8,128)(4,1)S(1)} %compare_and_fusion), kind=kOutput, calls=%fused_computation.210 | convolution fusion | flops 619727936 | bytes 40659584 | tf_op jit(solution)/shard_map/while/body/eval_jaxpr/hqk,khd->qhd/dot_general | solution.py:171
  434.3 35.2 %reduce-scatter.16.cloned.1.call-done = bf16[128,2176]{1,0:T(8,128)(2,1)} async-done(((bf16[2048,2176]{1,0:T(8,128)(2,1)}), bf16[128,2176]{1,0:T(8,128)(2,1)}) %reduce-scatter.16.cloned.1.call-update) | async-done | bytes 557072
  493.2 14.5 %reduce-scatter.18.cloned.1.call-done = bf16[136,1088]{1,0:T(8,128)(2,1)} async-done(((bf16[1088,1088]{1,0:T(8,128)(2,1)}), bf16[136,1088]{1,0:T(8,128)(2,1)}) %reduce-scatter.18.cloned.1.call-update) | async-done | bytes 295952
  507.7 58.7 %reduce-scatter.12.cloned.1.call-done = bf16[136,4352]{1,0:T(8,128)(2,1)} async-done(((bf16[1088,4352]{1,0:T(8,128)(2,1)}), bf16[136,4352]{1,0:T(8,128)(2,1)}) %reduce-scatter.12.cloned.1.call-update) | async-done | bytes 1183760 | tf_op jit(solution)/shard_map/reduce_scatter | solution.py:322
  566.4 62.2 %reduce-scatter.14.cloned.1.call-done = bf16[544,1088]{1,0:T(8,128)(2,1)} async-done(((bf16[4352,1088]{1,0:T(8,128)(2,1)}), bf16[544,1088]{1,0:T(8,128)(2,1)}) %reduce-scatter.14.cloned.1.call-update) | async-done | bytes 1183760 | tf_op jit(solution)/shard_map/reduce_scatter | solution.py:328
  628.6 49.1 %reduce-scatter.10.cloned.1.call-done = bf16[136,3264]{1,0:T(8,128)(2,1)} async-done(((bf16[1088,3264]{1,0:T(8,128)(2,1)}), bf16[136,3264]{1,0:T(8,128)(2,1)}) %reduce-scatter.10.cloned.1.call-update) | async-done | bytes 887824 | tf_op jit(solution)/shard_map/reduce_scatter | solution.py:313
  677.8 8.1 %fusion.56 = bf16[1,128,1088]{1,2,0:T(8,128)(2,1)} fusion(f32[128,1088]{0,1:T(8,128)S(1)} %get-tuple-element.157, bf16[4352,1088]{1,0:T(8,128)(2,1)} %all-gather.9.cloned.1.call-done, f32[1088]{0:T(1024)S(1)} %copy-done.13, f32[128,4352]{1,0:T(8,128)S(1)} %fusion.44), kind=kOutput, calls=%fused_computation.51 | convolution fusion | flops 1217585152 | bytes 12538112 | tf_op jit(solution)/shard_map/dot_general | solution.py:225
  701.6 41.4 %all-reduce.2 = (bf16[2,136]{1,0:T(2,128)(2,1)S(1)}, bf16[2,136]{1,0:T(2,128)(2,1)S(1)}, bf16[2,136]{1,0:T(2,128)(2,1)S(1)}, bf16[2,136]{1,0:T(2,128)(2,1)S(1)}, bf16[544]{0:T(1024)(128)(2,1)S(1)}) all-reduce(bf16[2,136]{1,0:T(2,128)(2,1)S(1)} %get-tuple-element.121, ...), channel_id=1, replica_groups=mesh['ctx'=16,'fsdp'=8] {'ctx'}, use_global_device_ids=true, to_apply=%region_21.22 | all-reduce | flops 1632 | bytes 6528 | tf_op jit(solution)/shard_map/psum | solution.py:335
  745.9 35.9 %all-reduce.6.cloned.1.call-done = (bf16[136,3264]{1,0:T(8,128)(2,1)}, bf16[136,1088]{1,0:T(8,128)(2,1)}, bf16[136,4352]{1,0:T(8,128)(2,1)}, bf16[544,1088]{1,0:T(8,128)(2,1)}) async-done(((bf16[136,3264]{1,0:T(8,128)(2,1)}, bf16[136,1088]{1,0:T(8,128)(2,1)}, bf16[136,4352]{1,0:T(8,128)(2,1)}, bf16[544,1088]{1,0:T(8,128)(2,1)}), (bf16[136,3264]{1,0:T(8,128)(2,1)}, bf16[136,1088]{1,0:T(8,128)(2,1)}, ...) | async-done | bytes 3551248 | tf_op jit(solution)/shard_map/psum | solution.py:337
  (170 shorter events, 127.6 us)
Async XLA Ops:
  7.2 20.2 %copy-start.1 = (bf16[1,128,1088]{1,2,0:T(8,128)(2,1)S(1)}, bf16[1,128,1088]{1,2,0:T(8,128)(2,1)}, u32[]{:S(2)}) copy-start(bf16[1,128,1088]{1,2,0:T(8,128)(2,1)} %param.13) | copy-start | bytes 835588
  7.2 101.9 %all-gather.5.cloned.1.call-start = ((), (), s32[]{:S(2)}) async-start(), calls=%async_computation.7 | async-start | bytes 21307392 | tf_op jit(solution)/shard_map/all_gather | solution.py:18
  12.5 186.3 %all-gather.7.cloned.1.call-start = ((), (), s32[]{:S(2)}) async-start(), calls=%async_computation.8 | async-start | bytes 9469952 | tf_op jit(solution)/shard_map/all_gather | solution.py:18
  109.1 8.5 %copy-start.15 = (u32[128]{0:T(128)S(1)}, u32[128]{0:T(128)}, u32[]{:S(2)}) copy-start(u32[128]{0:T(128)} %constant.189) | copy-start | bytes 1540
  109.1 9.8 %copy-start.14 = (bf16[544]{0:T(1024)(128)(2,1)S(1)}, bf16[544]{0:T(1024)(128)(2,1)}, u32[]{:S(2)}) copy-start(bf16[544]{0:T(1024)(128)(2,1)} %param.24) | copy-start | bytes 3268
  109.1 36.5 %copy-start.10 = (s32[32]{0:T(128)S(1)}, s32[32]{0:T(128)}, u32[]{:S(2)}) copy-start(s32[32]{0:T(128)} %param.15) | copy-start | bytes 388
  109.1 58.3 %copy-start.12 = (s32[1,2048]{1,0:T(1,128)S(1)}, s32[1,2048]{1,0:T(1,128)}, u32[]{:S(2)}) copy-start(s32[1,2048]{1,0:T(1,128)} %param.16) | copy-start | bytes 24580
  115.9 90.0 %copy-start.6 = (bf16[128,1088]{0,1:T(8,128)(2,1)}, bf16[128,1088]{0,1:T(8,128)(2,1)S(1)}, u32[]{:S(2)}) copy-start(bf16[128,1088]{0,1:T(8,128)(2,1)S(1)} %get-tuple-element.109) | copy-start | bytes 835588
  116.8 139.7 %all-gather.9.cloned.1.call-start = ((), (), s32[]{:S(2)}) async-start(), calls=%async_computation.9 | async-start | bytes 11280384 | tf_op jit(solution)/shard_map/all_gather | solution.py:108
  117.6 352.0 %reduce-scatter.16.cloned.1.call-start = ((), (), s32[]{:S(2)}) async-start(), calls=%async_computation.13 | async-start | bytes 9469952
  205.9 9.0 %copy-start = (bf16[1,2048,1088]{1,2,0:T(8,128)(2,1)}, bf16[1,2048,1088]{1,2,0:T(8,128)(2,1)S(1)}, u32[]{:S(2)}) copy-start(bf16[1,2048,1088]{1,2,0:T(8,128)(2,1)S(1)} %get-tuple-element.107) | copy-start | bytes 13369348
  263.5 11.1 %slice-start = ((s8[4456448]{0:T(1024)(128)(4,1)}), s8[4194304]{0:T(1024)(128)(4,1)S(1)}, s32[]{:S(2)}) async-start(s8[4456448]{0:T(1024)(128)(4,1)} %bitcast.144), calls=%async_computation.16 | async-start | bytes 8388608
  263.5 11.1 %slice-start.1 = ((s8[4456448]{0:T(1024)(128)(4,1)}), s8[262144]{0:T(1024)(128)(4,1)S(1)}, s32[]{:S(2)}) async-start(s8[4456448]{0:T(1024)(128)(4,1)} %bitcast.144), calls=%async_computation.17 | async-start | bytes 524288
  382.6 125.0 %reduce-scatter.18.cloned.1.call-start = ((), (), s32[]{:S(2)}) async-start(), calls=%async_computation.14 | async-start | bytes 2820096
  386.1 180.3 %reduce-scatter.12.cloned.1.call-start = ((), (), s32[]{:S(2)}) async-start(), calls=%async_computation.11 | async-start | bytes 10653696 | tf_op jit(solution)/shard_map/reduce_scatter | solution.py:322
  392.9 235.7 %reduce-scatter.14.cloned.1.call-start = ((), (), s32[]{:S(2)}) async-start(), calls=%async_computation.12 | async-start | bytes 11280384 | tf_op jit(solution)/shard_map/reduce_scatter | solution.py:328
  399.7 278.1 %reduce-scatter.10.cloned.1.call-start = ((), (), s32[]{:S(2)}) async-start(), calls=%async_computation.10 | async-start | bytes 8146944 | tf_op jit(solution)/shard_map/reduce_scatter | solution.py:313
  486.2 191.6 %copy-start.13 = (f32[1088]{0:T(1024)S(1)}, f32[1088]{0:T(1024)}, u32[]{:S(2)}) copy-start(f32[1088]{0:T(1024)} %get-tuple-element.92) | copy-start | bytes 13060
  488.5 197.8 %all-to-all-start.1 = ((bf16[8,2,272]{2,1,0:T(2,128)(2,1)}), bf16[8,2,272]{2,1,0:T(2,128)(2,1)S(1)}, u32[]{:S(2)}, u32[]{:S(2)}) async-start(bf16[8,2,272]{2,1,0:T(2,128)(2,1)} %reshape.513), calls=%async_computation.3 | async-start | bytes 24576 | tf_op jit(solution)/shard_map/all_to_all | solution.py:43
  492.9 288.9 %all-reduce.6.cloned.1.call-start = ((), (), s32[]{:S(2)}) async-start(), calls=%async_computation.15 | async-start | bytes 7311360 | tf_op jit(solution)/shard_map/psum | solution.py:337
  677.8 8.8 %copy-start.9 = (bf16[1,128,1088]{1,2,0:T(8,128)(2,1)S(1)}, bf16[1,128,1088]{1,2,0:T(8,128)(2,1)}, u32[]{:S(2)}) copy-start(bf16[1,128,1088]{1,2,0:T(8,128)(2,1)} %copy.32) | copy-start | bytes 835588
  686.6 9.6 %copy-start.3 = (f32[128,1088]{0,1:T(8,128)S(1)}, f32[128,1088]{0,1:T(8,128)}, u32[]{:S(2)}) copy-start(f32[128,1088]{0,1:T(8,128)} %copy-done.2) | copy-start | bytes 1671172
  692.9 8.7 %all-to-all-start = ((bf16[8,8,136]{2,1,0:T(8,128)(2,1)}), bf16[8,8,136]{2,1,0:T(8,128)(2,1)S(1)}, u32[]{:S(2)}, u32[]{:S(2)}) async-start(bf16[8,8,136]{2,1,0:T(8,128)(2,1)} %copy.28), calls=%async_computation | async-start | bytes 65536 | tf_op jit(solution)/shard_map/all_to_all | solution.py:43
  781.8 7.3 copy-start.7
  (5 other events, 25.8 us)
Sparse Core Ops, SparseCore 0:
  12.6 96.4 all-gather.4
  116.9 81.8 all-gather.6
  200.5 55.9 all-gather.8
  382.7 86.7 reduce-scatter.15
  472.5 35.1 reduce-scatter.17
  509.9 56.4 reduce-scatter.11
  568.8 59.7 reduce-scatter.13
  631.1 46.6 reduce-scatter.9
  682.2 99.6 all-reduce.5
where the time goes:
time: 808 us; the launch traced here: 798 us
  waiting for transfers between devices  381 us (47%)
  matrix products  184 us (23%)
  blocking collectives  80 us (10%)
  local copies, waits for them, and re-layouts  68.7 us (9%)
  other arithmetic  60.4 us (7%)
  between operations  15.4 us (2%)
  starting transfers between devices  8.31 us (1%)
    all_gather x2, waiting for transfers between devices, side_by_side(): out, at, done = (lax.all_gather(both, axis, axis=dim, tiled=True), 0, [])  113 us
    reduce_scatter x1, waiting for transfers between devices, per_device(): lax.psum_scatter(row_term(hidden_act, grad_flat).astype(jnp.bfloat16), 'f...  62.2 us
    reduce_scatter x1, waiting for transfers between devices, per_device(): lax.psum_scatter(row_term(normed_two_low, grad_pre).astype(jnp.bfloat16),...  58.7 us
    unnamed x54, local copies, waits for them, and re-layouts  52.3 us
    unnamed x11, waiting for transfers between devices  50.5 us
    reduce_scatter x1, waiting for transfers between devices, per_device(): lax.psum_scatter(row_term(normed_low, grad_qkv).astype(jnp.bfloat16), 'fs...  49.1 us
    psum x1, blocking collectives, per_device(): lax.psum(small_sums[0].astype(jnp.bfloat16), 'ctx').astype(jnp.float32)  41.4 us
    psum x1, waiting for transfers between devices, per_device(): lax.psum(qkv_shard, 'ctx').astype(jnp.float32)  35.9 us
  transfers between devices with their start and end apart: 11, of which 10 were waited for; matrix products, arithmetic and copies ran while one was open for 21% of the time, Pallas kernels for 0%

commit v1 on v0

v1 whole, which is shorter than its diff:
```python
import jax
import jax.numpy as jnp
from jax import lax
from jax.experimental import pallas as pl
from jax.experimental.layout import Layout, with_layout_constraint
from jax.experimental.pallas import tpu as pltpu
from jax.sharding import PartitionSpec as P

HEADS = 17
HD = 64
SPREAD = HEADS - 1
SIDE = 4
BLOCK_Q = 512
BLOCK_K = 256

epsilon = 1e-05
masked_value = -1e30

f32 = jnp.float32
bf16 = jnp.bfloat16


def contract(left, right, left_dims, right_dims):
    return lax.dot_general(
        left, right, ((left_dims, right_dims), ((), ())), preferred_element_type=f32
    )


def norm_scaled(values):
    row_mean = jnp.mean(values, axis=-1, keepdims=True)
    centred = values - row_mean
    variance = jnp.mean(centred * centred, axis=-1, keepdims=True)
    inverse = lax.rsqrt(variance + epsilon)
    return centred * inverse, inverse


def norm_backward(grad_norm, scaled, inverse, gain_row):
    grad_scaled = grad_norm * gain_row
    return inverse * (
        grad_scaled
        - jnp.mean(grad_scaled, axis=-1, keepdims=True)
        - scaled * jnp.mean(grad_scaled * scaled, axis=-1, keepdims=True)
    )


def rows_first(x):
    return with_layout_constraint(x, Layout(major_to_minor=tuple(range(x.ndim))))


def permuted(x, axis, pairs):
    return rows_first(lax.ppermute(rows_first(x), axis, pairs))


def from_z(x, d):
    pairs = [(y * SIDE + (z + d) % SIDE, y * SIDE + z) for y in range(SIDE) for z in range(SIDE)]
    return permuted(x, "ctx", pairs)


def from_y(x, d):
    pairs = [((y + d) % SIDE * SIDE + z, y * SIDE + z) for y in range(SIDE) for z in range(SIDE)]
    return permuted(x, "ctx", pairs)


def from_x(x, d):
    pairs = [((s + d) % SIDE * 2 + core, s * 2 + core) for s in range(SIDE) for core in range(2)]
    return permuted(x, "fsdp", pairs)


def from_core(x):
    return permuted(x, "fsdp", [(i ^ 1, i) for i in range(2 * SIDE)])


OTHERS = range(1, SIDE)


def gather_fsdp(x):
    near = [x] + [from_x(x, d) for d in OTHERS]
    return near + [from_core(part) for part in near]


def send_shards(paired):
    own, *others = paired
    return own, [from_x(others[d - 1], -d) for d in OTHERS]


def total_of(own, terms):
    for term in terms:
        own = own + term.astype(f32)
    return own


def exchange_sum(x, take):
    return total_of(x.astype(f32), [take(x, d) for d in OTHERS]).astype(bf16)


def after(x, *others):
    return lax.optimization_barrier((x, *others))[0]


def transposed(x):
    return x.astype(f32).T


def call(kernel, name, scalars, operands, outs, scratch=(), flops=0):
    def whole(shape):
        return pl.BlockSpec(shape, lambda i: (0,) * len(shape))

    moved = sum(x.size * x.dtype.itemsize for x in operands)
    moved += sum(x.size * jnp.dtype(x.dtype).itemsize for x in outs)
    return pl.pallas_call(
        kernel,
        grid=(1,),
        out_shape=tuple(outs),
        in_specs=[pl.BlockSpec(memory_space=pltpu.SMEM)] * len(scalars)
        + [whole(x.shape) for x in operands],
        out_specs=tuple(whole(x.shape) for x in outs),
        scratch_shapes=list(scratch),
        compiler_params=pltpu.CompilerParams(vmem_limit_bytes=60 * 1024 * 1024),
        cost_estimate=pl.CostEstimate(flops=flops, bytes_accessed=moved, transcendentals=0),
        name=name,
    )(*scalars, *operands)


def padded(width):
    return -(-width // 128) * 128


def widened(x):
    return jnp.pad(x, ((0, 0), (0, padded(x.shape[1]) - x.shape[1])))


def array(shape, dtype=f32):
    return jax.ShapeDtypeStruct(shape, dtype)


def masked_block(scores, first_key, low_row, high_row):
    key = lax.broadcasted_iota(jnp.int32, scores.shape, 0) + first_key
    allowed = key >= low_row
    if high_row is not None:
        allowed = allowed & (key <= high_row)
    return jnp.where(allowed, scores, masked_value)


def attend_rows(query, low_row, high_row, k_ref, vt_ref, scores_ref, keys, first_query):
    rows = query.shape[0]
    top = total = out = None
    for at in range(0, keys, BLOCK_K):
        here = slice(at, at + BLOCK_K)
        scores = contract(k_ref[here, :], query, (1,), (1,))
        crosses = at + BLOCK_K > first_query
        scores = masked_block(scores, at, low_row, high_row if crosses else None)
        scores_ref[here, :rows] = scores
        part = jnp.max(scores.reshape(-1, 8, rows), axis=0)
        top = part if top is None else jnp.maximum(top, part)
    top = jnp.max(top, axis=0, keepdims=True)
    for at in range(0, keys, BLOCK_K):
        here = slice(at, at + BLOCK_K)
        exponent = jnp.exp(scores_ref[here, :rows] - top)
        part = jnp.sum(exponent.reshape(-1, 8, rows), axis=0)
        total = part if total is None else total + part
        term = contract(vt_ref[:, here], exponent.astype(bf16), (1,), (0,))
        out = term if out is None else out + term
    total = jnp.sum(total, axis=0, keepdims=True)
    return out / total, top + jnp.log(total)


def forward_kernel(
    table_ref,
    at_ref,
    scaled_ref,
    weight_ref,
    gain_ref,
    shift_ref,
    bias_ref,
    starts_ref,
    own_ref,
    mixed_ref,
    mixed_last_ref,
    q_ref,
    k_ref,
    v_ref,
    k_last_ref,
    v_last_ref,
    q_last_ref,
    out_ref,
    log_ref,
    out_last_ref,
    log_last_ref,
    vt_ref,
    vt_last_ref,
    back_ref,
    scores_ref,
    all_last_ref,
):
    slots = mixed_ref.shape[0]
    rows = mixed_ref.shape[2]
    group = rows // 2
    seq_len = q_ref.shape[0]

    per_step = 2 * rows
    for first in range(0, seq_len, per_step):
        scaled = scaled_ref[first : first + per_step, :].astype(f32)
        normed = (scaled * gain_ref[...] + shift_ref[...]).astype(bf16)
        out = contract(normed, weight_ref[...], (1,), (0,)) + bias_ref[...]
        for n, dest in enumerate((q_ref, k_ref, v_ref, k_last_ref, v_last_ref, all_last_ref)):
            part = out[:, n * HD : (n + 1) * HD].astype(bf16)
            if n == 0 or n == 5:
                part = part * HD**-0.5
            if n == 5:
                dest[first : first + per_step, :] = part
                continue
            for k in range(per_step // group):
                at = pl.multiple_of(table_ref[first // group + k] * group, group)
                dest[pl.ds(at, group), :] = part[k * group : (k + 1) * group]
    q_last_ref[...] = all_last_ref[pl.ds(pl.multiple_of(at_ref[0] * rows, rows), rows), :]
    for at in range(0, seq_len, BLOCK_K):
        here = slice(at, at + BLOCK_K)
        vt_ref[:, here] = transposed(v_ref[here, :]).astype(bf16)
        vt_last_ref[:, here] = transposed(v_last_ref[here, :]).astype(bf16)

    out, log_total = attend_rows(
        q_last_ref[...],
        own_ref[0:1, :],
        own_ref[1:2, :],
        k_last_ref,
        vt_last_ref,
        scores_ref,
        seq_len,
        0,
    )
    out_last_ref[...] = out
    log_last_ref[...] = log_total
    mixed_last_ref[...] = out.astype(bf16)
    for first in range(0, seq_len, BLOCK_Q):
        here = slice(first, first + BLOCK_Q)
        high = lax.broadcasted_iota(jnp.int32, (1, BLOCK_Q), 1) + first
        out, log_total = attend_rows(
            q_ref[here, :],
            starts_ref[:, here],
            high,
            k_ref,
            vt_ref,
            scores_ref,
            first + BLOCK_Q,
            first,
        )
        out_ref[:, here] = out
        log_ref[:, here] = log_total
        back_ref[here, :] = out.T
    for j in range(slots):
        parts = []
        for half in range(2):
            at = pl.multiple_of(table_ref[2 * j + half] * group, group)
            parts.append(back_ref[pl.ds(at, group), :])
        mixed_ref[j] = jnp.concatenate(parts, axis=0).T.astype(bf16)


def backward_rows(
    query,
    grad,
    log_row,
    delta_row,
    low_row,
    high_row,
    k_ref,
    kt_ref,
    v_ref,
    gk_ref,
    gv_ref,
    keys,
    first_query,
):
    total = None
    for at in range(0, keys, BLOCK_K):
        here = slice(at, at + BLOCK_K)
        scores = contract(k_ref[here, :], query, (1,), (1,))
        crosses = at + BLOCK_K > first_query
        scores = masked_block(scores, at, low_row, high_row if crosses else None)
        probs = jnp.exp(scores - log_row)
        grad_probs = contract(v_ref[here, :], grad, (1,), (1,))
        grad_scores = (probs * (grad_probs - delta_row)).astype(bf16)
        gv_ref[here, :] += contract(probs.astype(bf16), grad, (1,), (0,))
        gk_ref[here, :] += contract(grad_scores, query, (1,), (0,))
        term = contract(kt_ref[:, here], grad_scores, (1,), (0,))
        total = term if total is None else total + term
    return total * HD**-0.5


def backward_kernel(
    table_ref,
    at_ref,
    recv_ref,
    grad_last_ref,
    starts_ref,
    own_ref,
    q_ref,
    k_ref,
    v_ref,
    k_last_ref,
    v_last_ref,
    q_last_ref,
    out_ref,
    log_ref,
    out_last_ref,
    log_last_ref,
    send_ref,
    gq_last_ref,
    rows_ref,
    grad_ref,
    kt_ref,
    kt_last_ref,
    gq_ref,
    gk_ref,
    gv_ref,
    gk_last_ref,
    gv_last_ref,
    packed_ref,
):
    slots = recv_ref.shape[0]
    group = recv_ref.shape[2] // 2
    seq_len = q_ref.shape[0]

    for j in range(slots):
        part = transposed(recv_ref[j]).astype(bf16)
        for half in range(2):
            at = pl.multiple_of(table_ref[2 * j + half] * group, group)
            grad_ref[pl.ds(at, group), :] = part[half * group : (half + 1) * group]
    for at in range(0, seq_len, BLOCK_K):
        here = slice(at, at + BLOCK_K)
        kt_ref[:, here] = transposed(k_ref[here, :]).astype(bf16)
        kt_last_ref[:, here] = transposed(k_last_ref[here, :]).astype(bf16)
    for ref in (gk_ref, gv_ref, gk_last_ref, gv_last_ref):
        ref[...] = jnp.zeros(ref.shape, f32)

    grad_last = grad_last_ref[...].astype(f32)
    delta = jnp.sum(out_last_ref[...] * grad_last, axis=0, keepdims=True)
    gq_last = backward_rows(
        q_last_ref[...],
        grad_last.T.astype(bf16),
        log_last_ref[...],
        delta,
        own_ref[0:1, :],
        own_ref[1:2, :],
        k_last_ref,
        kt_last_ref,
        v_last_ref,
        gk_last_ref,
        gv_last_ref,
        seq_len,
        0,
    ).astype(bf16)
    gq_last_ref[...] = gq_last

    for first in range(0, seq_len, BLOCK_Q):
        here = slice(first, first + BLOCK_Q)
        high = lax.broadcasted_iota(jnp.int32, (1, BLOCK_Q), 1) + first
        grad = grad_ref[here, :]
        delta = jnp.sum(out_ref[:, here] * transposed(grad), axis=0, keepdims=True)
        total = backward_rows(
            q_ref[here, :],
            grad,
            log_ref[:, here],
            delta,
            starts_ref[:, here],
            high,
            k_ref,
            kt_ref,
            v_ref,
            gk_ref,
            gv_ref,
            first + BLOCK_Q,
            first,
        )
        gq_ref[here, :] = total.T

    for at in range(0, seq_len, BLOCK_K):
        here = slice(at, at + BLOCK_K)
        packed_ref[here, :] = jnp.concatenate(
            [ref[here, :] for ref in (gq_ref, gk_ref, gv_ref, gk_last_ref, gv_last_ref)]
            + [jnp.zeros((BLOCK_K, HD), f32)],
            axis=1,
        ).astype(bf16)
    last_rows = transposed(gq_last).astype(bf16)
    for half in range(2):
        at = pl.multiple_of(table_ref[2 * at_ref[0] + half] * group, group)
        packed_ref[pl.ds(at, group), 5 * HD :] = last_rows[half * group : (half + 1) * group]
    for n in range(2 * slots):
        at = pl.multiple_of(table_ref[n] * group, group)
        rows_ref[n * group : (n + 1) * group, :] = packed_ref[pl.ds(at, group), :]
    for j in range(slots):
        parts = []
        for half in range(2):
            at = pl.multiple_of(table_ref[2 * j + half] * group, group)
            parts.append(packed_ref[pl.ds(at, group), :])
        block = transposed(jnp.concatenate(parts, axis=0)).astype(bf16)
        send_ref[j] = block[: 5 * HD]


def attention_forward(table, at, scaled, weight, gain, shift, bias, starts, own):
    slots, rows = SIDE * SIDE, own.shape[1]
    seq_len = slots * rows
    saved = array((seq_len, HD), bf16)
    return call(
        forward_kernel,
        "attention_forward",
        (table, at),
        (scaled, weight, gain, shift, bias, starts, own),
        (
            array((slots, HD, rows), bf16),
            array((HD, rows), bf16),
            saved,
            saved,
            saved,
            saved,
            saved,
            array((rows, HD), bf16),
            array((HD, seq_len)),
            array((1, seq_len)),
            array((HD, rows)),
            array((1, rows)),
        ),
        (
            pltpu.VMEM((HD, seq_len), bf16),
            pltpu.VMEM((HD, seq_len), bf16),
            pltpu.VMEM((seq_len, HD), f32),
            pltpu.VMEM((seq_len, BLOCK_Q), f32),
            pltpu.VMEM((seq_len, HD), bf16),
        ),
        flops=8 * 10**9,
    )


def attention_backward(table, at, recv, grad_last, starts, own, saved):
    slots, _, rows = recv.shape
    seq_len = slots * rows
    wide = pltpu.VMEM((seq_len, HD), f32)
    return call(
        backward_kernel,
        "attention_backward",
        (table, at),
        (recv, grad_last, starts, own, *saved),
        (
            array((slots, 5 * HD, rows), bf16),
            array((HD, rows), bf16),
            array((seq_len, 6 * HD), bf16),
        ),
        (
            pltpu.VMEM((seq_len, HD), bf16),
            pltpu.VMEM((HD, seq_len), bf16),
            pltpu.VMEM((HD, seq_len), bf16),
            wide,
            wide,
            wide,
            wide,
            wide,
            pltpu.VMEM((seq_len, 6 * HD), bf16),
        ),
        flops=12 * 10**9,
    )


def hidden_kernel(at_ref, values_ref, *refs):
    count = 2 * SIDE
    grads, refs = refs[:count], refs[count:]
    (
        up_ref,
        down_ref,
        gain_ref,
        shift_ref,
        bias_ref,
        act_ref,
        pre_ref,
        near_ref,
        far_ref,
    ) = refs
    rows = grads[0].shape[0]
    slope = (2 / jnp.pi) ** 0.5
    for n in reversed(range(0, count, 2)):
        here = slice(n * rows, (n + 2) * rows)
        places = [shard_at(at_ref, (n + k) % SIDE, n // SIDE) for k in range(2)]
        scaled = jnp.concatenate(
            [values_ref[pl.ds(pl.multiple_of(at * rows, rows), rows), :] for at in places], axis=0
        ).astype(f32)
        normed = (scaled * gain_ref[...] + shift_ref[...]).astype(bf16)
        pre = contract(normed, up_ref[...], (1,), (0,)) + bias_ref[...]
        square = pre * pre
        bend = jnp.tanh(slope * pre * (1 + 0.044715 * square))
        half = 0.5 * (1 + bend)
        act_ref[here, :] = (pre * half).astype(bf16)
        steep = half + 0.5 * pre * (1 - bend * bend) * slope * (1 + 3 * 0.044715 * square)
        grad = jnp.concatenate([grads[n][...], grads[n + 1][...]], axis=0)
        grad_pre = (contract(grad, down_ref[...], (1,), (1,)) * steep).astype(bf16)
        pre_ref[here, :] = grad_pre
        part = widened(contract(grad_pre, up_ref[...], (1,), (1,)))
        for k in range(2):
            if n < SIDE:
                near_ref[n + k] = part[k * rows : (k + 1) * rows]
            else:
                far_ref[n + k - SIDE] = part[k * rows : (k + 1) * rows].astype(bf16)


def hidden_pass(at, values, grads, up_cols, w_down, gain, shift, bias):
    rows, width = grads[0].shape
    total, hidden = 2 * SIDE * rows, up_cols.shape[1]
    return call(
        hidden_kernel,
        "hidden_pass",
        (at,),
        (values, *grads, up_cols, w_down, gain, shift, bias),
        (
            array((total, hidden), bf16),
            array((total, hidden), bf16),
            array((SIDE, rows, padded(width))),
            array((SIDE, rows, padded(width)), bf16),
        ),
        flops=6 * total * hidden * width,
    )


def hidden_grads_kernel(at_ref, values_ref, *refs):
    count = 2 * SIDE
    grads, refs = refs[:count], refs[count:]
    (
        act_ref,
        pre_ref,
        down_ref,
        near_ref,
        far_ref,
        grad_down_ref,
        moment_ref,
        ordered_ref,
        grads_ref,
    ) = refs
    rows = grads[0].shape[0]
    half = SIDE * rows
    for n in range(count):
        at = pl.multiple_of(shard_at(at_ref, n % SIDE, n // SIDE) * rows, rows)
        ordered_ref[n * rows : (n + 1) * rows, :] = values_ref[pl.ds(at, rows), :]
        grads_ref[n * rows : (n + 1) * rows, :] = grads[n][...]
    near = widened(contract(act_ref[:half, :], down_ref[...], (1,), (0,)))
    far = widened(contract(act_ref[half:, :], down_ref[...], (1,), (0,))).astype(bf16)
    for n in range(SIDE):
        near_ref[n] = near[n * rows : (n + 1) * rows]
        far_ref[n] = far[n * rows : (n + 1) * rows]
    grad_down_ref[...] = contract(act_ref[...], grads_ref[...], (0,), (0,)).astype(bf16)
    moment = contract(ordered_ref[...], pre_ref[...], (0,), (0,))
    shard = moment.shape[0] // count
    fill = moment_ref.shape[1] - shard
    totals = jnp.sum(pre_ref[...].astype(f32), axis=0, keepdims=True)
    row = lax.broadcasted_iota(jnp.int32, (fill, moment.shape[1]), 0)
    tail = jnp.where(row == 0, totals, 0.0)
    for f in range(count):
        moment_ref[f] = jnp.concatenate(
            [moment[f * shard : (f + 1) * shard], tail], axis=0
        ).astype(bf16)


def hidden_grads(at, values, grads, act, pre, w_down):
    rows, width = grads[0].shape
    total, hidden = act.shape
    count = 2 * SIDE
    shard = width // count
    return call(
        hidden_grads_kernel,
        "hidden_grads",
        (at,),
        (values, *grads, act, pre, w_down),
        (
            array((SIDE, rows, padded(width))),
            array((SIDE, rows, padded(width)), bf16),
            array((hidden, width), bf16),
            array((count, shard // 16 * 16 + 16, hidden), bf16),
        ),
        (pltpu.VMEM((total, width), bf16), pltpu.VMEM((total, width), bf16)),
        flops=6 * total * hidden * width,
    )


def pair_kernel(near_ref, far_ref, own_ref, *others):
    own_ref[...] = near_ref[0] + far_ref[0].astype(f32)
    for n, ref in enumerate(others, 1):
        ref[...] = (near_ref[n] + far_ref[n].astype(f32)).astype(bf16)


def pair_up(near, far):
    count, rows, cols = near.shape
    return call(
        pair_kernel,
        "pair_up",
        (),
        (near, far),
        (array((rows, cols)), *[array((rows, cols), bf16)] * (count - 1)),
    )


def shard_at(at_ref, dx, dcore):
    return (at_ref[0] + dx) % SIDE * 2 + (at_ref[1] + dcore) % 2


def attend_out_kernel(at_ref, recv_ref, last_ref, tokens_ref, bias_ref, *refs):
    blocks, refs = refs[: 2 * SIDE], refs[2 * SIDE :]
    mixed_ref, residual_ref, scaled_ref, scaled_low_ref, inverse_ref, rows_ref = refs
    slots, size, _ = recv_ref.shape
    for n in range(slots):
        rows_ref[n * size : (n + 1) * size, :] = recv_ref[n].astype(f32)
    rows_ref[slots * size :, :] = last_ref[...].astype(f32)
    mixed_ref[...] = rows_ref[...].astype(bf16)
    shard = blocks[0].shape[0]
    residual = tokens_ref[...].astype(f32) + bias_ref[...]
    for n, block_ref in enumerate(blocks):
        at = pl.multiple_of(shard_at(at_ref, n % SIDE, n // SIDE) * shard, 8)
        part = rows_ref[pl.ds(at, shard), :].astype(bf16)
        residual = residual + contract(part, block_ref[...], (0,), (0,))
    residual_ref[...] = residual
    scaled, inverse = norm_scaled(residual)
    scaled_ref[...] = scaled
    scaled_low_ref[...] = scaled.astype(bf16)
    inverse_ref[...] = inverse


def attend_out(at, recv, last, tokens, bias, blocks):
    rows, width = tokens.shape
    return call(
        attend_out_kernel,
        "attend_out",
        (at,),
        (recv, last, tokens, bias, *blocks),
        (
            array((width, rows), bf16),
            array((rows, width)),
            array((rows, width)),
            array((rows, width), bf16),
            array((rows, 1)),
        ),
        (pltpu.VMEM((width, rows), f32),),
        flops=2 * rows * width * width,
    )


def mixed_grads_kernel(at_ref, *refs):
    own_ref, terms, refs = refs[0], refs[1:SIDE], refs[SIDE:]
    grad_ref, scaled_ref, inverse_ref, gain_ref = refs[:4]
    blocks, refs = refs[4 : 4 + 2 * SIDE], refs[4 + 2 * SIDE :]
    residual_ref, low_ref, send_ref, last_ref, rows_ref = refs
    width = grad_ref.shape[1]
    grad_norm = total_of(own_ref[...], [ref[...] for ref in terms])[:, :width]
    residual = grad_ref[...].astype(f32) + norm_backward(
        grad_norm, scaled_ref[...], inverse_ref[...], gain_ref[...]
    )
    residual_ref[...] = residual
    low = residual.astype(bf16)
    low_ref[...] = low
    shard = blocks[0].shape[0]
    for n, block_ref in enumerate(blocks):
        at = pl.multiple_of(shard_at(at_ref, n % SIDE, n // SIDE) * shard, 8)
        rows_ref[pl.ds(at, shard), :] = contract(block_ref[...], low, (1,), (1,))
    slots, size, _ = send_ref.shape
    for n in range(slots):
        send_ref[n] = rows_ref[n * size : (n + 1) * size, :].astype(bf16)
    last_ref[...] = rows_ref[slots * size :, :].astype(bf16)


def mixed_grads(at, own, terms, grad, scaled, inverse, gain, blocks):
    rows, width = grad.shape
    return call(
        mixed_grads_kernel,
        "mixed_grads",
        (at,),
        (own, *terms, grad, scaled, inverse, gain, *blocks),
        (
            array((rows, width)),
            array((rows, width), bf16),
            array((SPREAD, HD, rows), bf16),
            array((HD, rows), bf16),
        ),
        (pltpu.VMEM((width, rows), f32),),
        flops=2 * rows * width * width,
    )


def give_shards(at_ref, rows_ref, tail, near_ref, far_ref):
    shard = rows_ref.shape[0] // (2 * SIDE)
    for dest_ref, dcore in ((near_ref, 0), (far_ref, 1)):
        for dx in range(SIDE):
            at = pl.multiple_of(shard_at(at_ref, dx, dcore) * shard, 8)
            block = jnp.concatenate([rows_ref[pl.ds(at, shard), :], tail], axis=0)
            dest_ref[dx] = widened(block).astype(dest_ref.dtype)


def out_grads_kernel(at_ref, mixed_ref, low_ref, grad_ref, near_ref, far_ref, rows_ref):
    rows_ref[...] = contract(mixed_ref[...], low_ref[...], (1,), (0,))
    shard = rows_ref.shape[0] // (2 * SIDE)
    shape = (near_ref.shape[1] - shard, rows_ref.shape[1])
    row = lax.broadcasted_iota(jnp.int32, shape, 0)
    first = jnp.sum(low_ref[...].astype(f32), axis=0, keepdims=True)
    second = jnp.sum(grad_ref[...].astype(f32), axis=0, keepdims=True)
    tail = jnp.where(row == 0, first, jnp.where(row == 1, second, 0.0))
    give_shards(at_ref, rows_ref, tail, near_ref, far_ref)


def out_grads(at, mixed, low, grad):
    rows, width = low.shape
    tall = width // (2 * SIDE) // 16 * 16 + 16
    return call(
        out_grads_kernel,
        "out_grads",
        (at,),
        (mixed, low, grad),
        (array((SIDE, tall, padded(width))), array((SIDE, tall, padded(width)), bf16)),
        (pltpu.VMEM((width, width), f32),),
        flops=2 * rows * width * width,
    )


def projection_grads_kernel(at_ref, scaled_ref, grads_ref, near_ref, far_ref, rows_ref):
    step = 512
    sums = None
    for first in range(0, scaled_ref.shape[0], step):
        grads = grads_ref[first : first + step, :]
        term = contract(scaled_ref[first : first + step, :], grads, (0,), (0,))
        part = jnp.sum(grads.astype(f32), axis=0, keepdims=True)
        if first == 0:
            rows_ref[...] = term
            sums = part
        else:
            rows_ref[...] += term
            sums = sums + part
    shard = rows_ref.shape[0] // (2 * SIDE)
    shape = (near_ref.shape[1] - shard, rows_ref.shape[1])
    row = lax.broadcasted_iota(jnp.int32, shape, 0)
    give_shards(at_ref, rows_ref, jnp.where(row == 0, sums, 0.0), near_ref, far_ref)


def projection_grads(at, scaled, grads):
    seq_len, width = scaled.shape
    cols = grads.shape[1]
    tall = width // (2 * SIDE) // 16 * 16 + 16
    return call(
        projection_grads_kernel,
        "projection_grads",
        (at,),
        (scaled, grads),
        (array((SIDE, tall, cols)), array((SIDE, tall, cols), bf16)),
        (pltpu.VMEM((width, cols), f32),),
        flops=2 * seq_len * width * cols,
    )


def finish_up_kernel(at_ref, moment_ref, w_ref, gain_ref, shift_ref, *refs):
    grad_ref, gains_ref, shifts_ref, sums_ref = refs
    count, _, cols = moment_ref.shape
    shard = w_ref.shape[0]
    gains = jnp.zeros((shard, cols), f32)
    shifts = jnp.zeros((shard, cols), f32)
    for s in range(count):
        moment = moment_ref[s].astype(f32)
        rows, sums = moment[:shard], moment[shard : shard + 1]
        weight = w_ref[:, s * cols : (s + 1) * cols].astype(f32)
        grad_ref[:, s * cols : (s + 1) * cols] = gain_ref[...] * rows + shift_ref[...] * sums
        gains += weight * rows
        shifts += weight * sums
    gains_ref[...] = jnp.sum(gains, axis=1, keepdims=True)
    shifts_ref[...] = jnp.sum(shifts, axis=1, keepdims=True)
    sums_ref[...] = moment_ref[at_ref[0]][shard : shard + 1].astype(f32)


def finish_up(at, moments, weight, gain, shift):
    shard = weight.shape[0]
    return call(
        finish_up_kernel,
        "finish_up",
        (at,),
        (moments, weight, gain, shift),
        (
            array(weight.shape),
            array((shard, 1)),
            array((shard, 1)),
            array((1, moments.shape[2])),
        ),
    )


def finish_qkv_kernel(head_ref, w_ref, gain_ref, shift_ref, *refs):
    grad_ref, gains_ref, shifts_ref, sums_ref = refs
    shard = w_ref.shape[0]
    last = head_ref[0, :, 3 * HD :].astype(f32)
    for h in range(1, SPREAD):
        last = last + head_ref[h, :, 3 * HD :].astype(f32)

    def unit(u):
        n, h = u // HEADS, u % HEADS
        if h < SPREAD:
            return head_ref[h, :, n * HD : (n + 1) * HD].astype(f32)
        at = (2, 0, 1)[n] * HD
        return last[:, at : at + HD]

    units = 3 * HEADS
    gains = jnp.zeros((shard, 2 * HD), f32)
    shifts = jnp.zeros((shard, 2 * HD), f32)
    for u in range(0, units, 2):
        if u + 1 < units:
            moment = jnp.concatenate([unit(u), unit(u + 1)], axis=1)
        else:
            moment = unit(u)
        size = moment.shape[1]
        rows, sums = moment[:shard], moment[shard : shard + 1]
        cols = slice(u * HD, u * HD + size)
        weight = w_ref[:, cols].astype(f32)
        grad_ref[:, cols] = gain_ref[...] * rows + shift_ref[...] * sums
        sums_ref[:, cols] = sums
        if size == 2 * HD:
            gains += weight * rows
            shifts += weight * sums
        else:
            more_gains = jnp.sum(weight * rows, axis=1, keepdims=True)
            more_shifts = jnp.sum(weight * sums, axis=1, keepdims=True)
    gains_ref[...] = jnp.sum(gains, axis=1, keepdims=True) + more_gains
    shifts_ref[...] = jnp.sum(shifts, axis=1, keepdims=True) + more_shifts


def finish_qkv(heads, weight, gain, shift):
    shard, total_cols = weight.shape
    return call(
        finish_qkv_kernel,
        "finish_qkv",
        (),
        (heads, weight, gain, shift),
        (array(weight.shape), array((shard, 1)), array((shard, 1)), array((1, total_cols))),
    )


def per_device(
    tokens,
    grad_out,
    group_table,
    doc_ids,
    norm_gains,
    norm_biases,
    w_qkv,
    qv_bias,
    w_out,
    out_biases,
    w_up,
    up_bias,
    w_down,
):
    _, own_rows, width = tokens.shape
    seq_len = doc_ids.shape[1]
    ctx_count = lax.axis_size("ctx")
    fsdp_count = lax.axis_size("fsdp")
    ctx_at = lax.axis_index("ctx")
    fsdp_at = lax.axis_index("fsdp")
    group_rows = seq_len // (2 * ctx_count)
    shard = width // fsdp_count
    ff_slice = w_down.shape[0]

    shard_place = jnp.stack([fsdp_at // 2, fsdp_at % 2])
    ctx_place = ctx_at[None]

    tokens_float = tokens[0].astype(f32)
    scaled_one, inverse_one = norm_scaled(tokens_float)
    scaled_seq = lax.all_gather(scaled_one.astype(bf16), "ctx", axis=0, tiled=True)

    def head_columns(x, n, head):
        return lax.dynamic_slice_in_dim(x, n * width + head * HD, HD, axis=x.ndim - 1)

    weight_cols = jnp.concatenate(
        [head_columns(w_qkv, n, ctx_at) for n in range(3)]
        + [head_columns(w_qkv, n, SPREAD) for n in (1, 2, 0)],
        axis=1,
    )
    small = jnp.concatenate([norm_gains, norm_biases, qv_bias, out_biases], axis=0)
    first_cols = lax.all_gather(
        after(jnp.concatenate([weight_cols, small.T], axis=1), scaled_one),
        "fsdp",
        axis=0,
        tiled=True,
    )
    head_weight = first_cols[:, : 6 * HD]
    small_full = first_cols[:, 6 * HD :].T.astype(f32)
    gains, biases, qv_full, outb = (small_full[2 * n : 2 * n + 2] for n in range(4))
    no_bias = jnp.zeros((HD,), f32)
    head_bias = jnp.concatenate(
        [
            head_columns(qv_full[0], 0, ctx_at),
            no_bias,
            head_columns(qv_full[1], 0, ctx_at),
            no_bias,
            head_columns(qv_full[1], 0, SPREAD),
            head_columns(qv_full[0], 0, SPREAD),
        ]
    )[None]
    out_blocks = gather_fsdp(after(w_out, first_cols))
    grad_all = gather_fsdp(after(grad_out[0], first_cols))
    up_cols = lax.all_to_all(
        after(w_up, first_cols).reshape(shard, fsdp_count, ff_slice).transpose(1, 0, 2),
        "fsdp",
        0,
        0,
        tiled=True,
    ).reshape(width, ff_slice)
    full_qkv = lax.all_gather(
        after(w_qkv, scaled_seq, up_cols, *grad_all, *out_blocks), "fsdp", axis=0, tiled=True
    )

    slot = jnp.arange(2 * ctx_count, dtype=jnp.int32)
    order = jnp.sum(jnp.where(group_table[None] == slot[:, None], slot[None], 0), axis=1)
    docs = doc_ids.reshape(2 * ctx_count, group_rows)[order].reshape(1, seq_len)
    first_one = jnp.sum((docs < 1).astype(jnp.int32))
    first_two = jnp.sum((docs < 2).astype(jnp.int32))

    def start_of(ids):
        return jnp.where(ids >= 2, first_two, jnp.where(ids >= 1, first_one, 0))

    starts = start_of(docs)
    own_groups = lax.dynamic_slice_in_dim(group_table, 2 * ctx_at, 2)
    own_pos = (
        own_groups[:, None] * group_rows + jnp.arange(group_rows, dtype=jnp.int32)[None, :]
    ).reshape(1, own_rows)
    own_docs = lax.dynamic_slice_in_dim(doc_ids, ctx_at * own_rows, own_rows, axis=1)
    own = jnp.concatenate([start_of(own_docs), own_pos], axis=0)

    mixed_send, mixed_last, *saved = attention_forward(
        group_table,
        ctx_place,
        scaled_seq,
        head_weight,
        gains[:1],
        biases[:1],
        head_bias,
        starts,
        own,
    )
    mixed_recv = lax.all_to_all(mixed_send, "ctx", 0, 0, tiled=True)
    mixed, residual, scaled_two, scaled_two_low, inverse_two = attend_out(
        shard_place, mixed_recv, mixed_last, tokens[0], outb[:1], out_blocks
    )
    scaled_all = lax.all_gather(
        after(scaled_two_low, full_qkv), "fsdp", axis=0, tiled=True
    )
    hidden_act, grad_pre, near, far = hidden_pass(
        shard_place,
        scaled_all,
        grad_all,
        up_cols,
        w_down,
        gains[1:],
        biases[1:],
        up_bias.astype(f32)[None],
    )
    own_term, terms = send_shards(pair_up(near, from_core(far)))
    block_near, block_far, down_part, up_moment = hidden_grads(
        shard_place, scaled_all, grad_all, hidden_act, grad_pre, w_down
    )
    down_sum, up_sum = lax.psum((down_part, up_moment), "ctx")
    block_recv = from_core(after(block_far, own_term))
    grad_residual, grad_attended, grad_mixed, grad_mixed_last = mixed_grads(
        shard_place,
        after(own_term, down_part),
        terms,
        grad_out[0],
        scaled_two,
        inverse_two,
        gains[1:],
        out_blocks,
    )
    grad_recv = lax.all_to_all(grad_mixed, "ctx", 0, 0, tiled=True)
    block_pairs = pair_up(after(block_near, grad_attended), block_recv)
    out_near, out_far = out_grads(shard_place, mixed, grad_attended, grad_out[0])
    out_pairs = pair_up(out_near, from_core(out_far))
    block_own, block_terms = send_shards(block_pairs)
    out_own, out_terms = send_shards(out_pairs)

    grad_send, gq_last, grad_rows = attention_backward(
        group_table,
        ctx_place,
        after(grad_recv, block_own, out_own),
        grad_mixed_last,
        starts,
        own,
        saved,
    )
    grad_back = lax.all_to_all(grad_send, "ctx", 0, 0, tiled=True)

    qkv_near, qkv_far = projection_grads(shard_place, scaled_seq, grad_rows)
    qkv_own, qkv_terms = send_shards(pair_up(qkv_near, from_core(qkv_far)))
    qkv_part = total_of(qkv_own, qkv_terms).astype(bf16)
    qkv_heads = lax.all_to_all(
        jnp.broadcast_to(qkv_part[None], (ctx_count, *qkv_part.shape)), "ctx", 0, 0, tiled=True
    )
    block_out = (
        total_of(residual + block_own[:, :width], [term[:, :width] for term in block_terms])
        + outb[1]
    ).astype(bf16)
    out_sum = total_of(out_own, out_terms).astype(bf16)
    out_sum = exchange_sum(exchange_sum(out_sum, from_z), from_y)

    def rows_of(n, last):
        return jnp.concatenate(
            [grad_back[:, n * HD : (n + 1) * HD].reshape(SPREAD * HD, own_rows), last], axis=0
        )

    last_sums = jnp.sum(grad_back[:, 3 * HD :].astype(f32), axis=0).astype(bf16)
    grad_qkv = jnp.concatenate(
        [rows_of(0, gq_last), rows_of(1, last_sums[:HD]), rows_of(2, last_sums[HD:])], axis=0
    )
    grad_normed = contract(grad_qkv, full_qkv, (0,), (1,))
    grad_tokens = (
        grad_residual + norm_backward(grad_normed, scaled_one, inverse_one, gains[0])
    ).astype(bf16)

    own_gains = norm_gains.astype(f32)[:, :, None]
    own_biases = norm_biases.astype(f32)[:, :, None]
    down_sum, up_sum = lax.optimization_barrier((down_sum, up_sum, qkv_part, out_sum))[:2]
    up_all = lax.all_to_all(up_sum, "fsdp", 0, 0, tiled=True)
    grad_w_up, up_gain, up_shift, grad_upb = finish_up(
        fsdp_at[None], up_all, w_up, own_gains[1], own_biases[1]
    )
    grad_w_qkv, qkv_gain, qkv_shift, qkv_sums = finish_qkv(
        qkv_heads, w_qkv, own_gains[0], own_biases[0]
    )
    grad_qv = jnp.concatenate(
        [
            lax.dynamic_slice_in_dim(qkv_sums, fsdp_at * shard, shard, axis=1),
            lax.dynamic_slice_in_dim(qkv_sums, 2 * width + fsdp_at * shard, shard, axis=1),
        ],
        axis=0,
    )
    grad_outb = lax.dynamic_slice(out_sum, (shard, fsdp_at * shard), (2, shard)).astype(f32)
    return (
        block_out[None],
        grad_tokens[None],
        jnp.stack([qkv_gain[:, 0], up_gain[:, 0]]),
        jnp.stack([qkv_shift[:, 0], up_shift[:, 0]]),
        grad_w_qkv,
        grad_qv,
        out_sum[:shard, :width].astype(f32),
        grad_outb,
        grad_w_up,
        grad_upb[0],
        down_sum.astype(f32),
    )


def solution(mesh):
    return jax.shard_map(
        per_device,
        mesh=mesh,
        in_specs=(
            P("fsdp", "ctx", None),
            P("fsdp", "ctx", None),
            P(),
            P("fsdp", None),
            P(None, "fsdp"),
            P(None, "fsdp"),
            P("fsdp", None),
            P(None, "fsdp"),
            P("fsdp", None),
            P(None, "fsdp"),
            P("fsdp", None),
            P("fsdp"),
            P("fsdp", None),
        ),
        out_specs=(
            P("fsdp", "ctx", None),
            P("fsdp", "ctx", None),
            P(None, "fsdp"),
            P(None, "fsdp"),
            P("fsdp", None),
            P(None, "fsdp"),
            P("fsdp", None),
            P(None, "fsdp"),
            P("fsdp", None),
            P("fsdp"),
            P("fsdp", None),
        ),
        check_vma=False,
    )
```

time: 808 us -> 406 us (0.50)
  waiting for transfers between devices: 381 us -> 137 us
  matrix products: 184 us -> 6 us
  Pallas kernels: 0 us -> 89 us
  starting transfers between devices: 8.31 us -> 83.9 us
  blocking collectives: 80 us -> 15.2 us
  other arithmetic: 60.4 us -> 21 us
  local copies, waits for them, and re-layouts: 68.7 us -> 31.6 us
    dot_general x18 -> x1, matrix products: 184 us -> 6 us  [contract(): lax.dot_general(left, right, ((left_dims, right_dims), ((), ())), preferr...]
    reduce_scatter x3 -> x0, waiting for transfers between devices: 170 us -> none  [the longest x1 62.2 us: per_device(): lax.psum_scatter(row_term(hidden_act, grad_flat).astype(jnp.bfloat16), 'f...]
    all_gather x3, waiting for transfers between devices: 120 us -> 29.3 us  [the longest x1 27.4 us: per_device(): lax.all_gather(after(scaled_two_low, full_qkv), 'fsdp', axis=0, tiled=True)]
    pallas_call x0 -> x14, Pallas kernels: none -> 89 us  [call(): pl.pallas_call(kernel, grid=(1,), out_shape=tuple(outs), in_specs=[pl.Blo...]
    ppermute x0 -> x36, waiting for transfers between devices: none -> 52.7 us  [permuted(): return rows_first(lax.ppermute(rows_first(x), axis, pairs))]
    unnamed x11 -> x4, waiting for transfers between devices: 50.5 us -> 0.56 us
    ppermute x0 -> x36, starting transfers between devices: none -> 46.7 us  [permuted(): return rows_first(lax.ppermute(rows_first(x), axis, pairs))]
    psum x1 -> x0, blocking collectives: 41.4 us -> none  [per_device(): lax.psum(small_sums[0].astype(jnp.bfloat16), 'ctx').astype(jnp.float32)]
  transfers between devices with their start and end apart: 11 -> 46, of which waited for: 10 -> 18; matrix products, arithmetic and copies ran while one was open for 21% -> 11% of each run, Pallas kernels for 0% -> 15%
where the time goes in v1:
time: 406 us; the launch traced here: 399 us
  waiting for transfers between devices  137 us (34%)
  Pallas kernels  89 us (22%)
  starting transfers between devices  83.9 us (21%)
  local copies, waits for them, and re-layouts  31.6 us (8%)
  other arithmetic  21 us (5%)
  blocking collectives  15.2 us (4%)
  between operations  14.7 us (4%)
  matrix products  6 us (1%)
    pallas_call x14, Pallas kernels, call(): pl.pallas_call(kernel, grid=(1,), out_shape=tuple(outs), in_specs=[pl.Blo...  89 us
    ppermute x36, waiting for transfers between devices, permuted(): return rows_first(lax.ppermute(rows_first(x), axis, pairs))  52.7 us
    ppermute x36, starting transfers between devices, permuted(): return rows_first(lax.ppermute(rows_first(x), axis, pairs))  46.7 us
    all_gather x1, waiting for transfers between devices, per_device(): lax.all_gather(after(scaled_two_low, full_qkv), 'fsdp', axis=0, tiled=True)  27.4 us
    psum x1, waiting for transfers between devices, per_device(): down_sum, up_sum = lax.psum((down_part, up_moment), 'ctx')  26.2 us
    unnamed x107, local copies, waits for them, and re-layouts  15.9 us
    all_gather x1, blocking collectives, per_device(): lax.all_gather(after(jnp.concatenate([weight_cols, small.T], axis=1), sca...  15.2 us
    all_to_all x1, waiting for transfers between devices, per_device(): up_all = lax.all_to_all(up_sum, 'fsdp', 0, 0, tiled=True)  12.7 us
  transfers between devices with their start and end apart: 46, of which 18 were waited for; matrix products, arithmetic and copies ran while one was open for 11% of the time, Pallas kernels for 15%

profile of v1, /device:TPU:0, one launch (start us, length us, event | category | flops | bytes accessed | tf_op | source)
XLA Modules:
  0.0 398.8 jit_solution(15479829919898562055)
XLA Ops:
  11.0 15.2 %all_gather.13 = bf16[1088,392]{1,0:T(8,128)(2,1)} all-gather(bf16[136,392]{1,0:T(8,128)(2,1)S(1)} %concatenate.19), channel_id=1, replica_groups=mesh['ctx'=16,'fsdp'=8] {'fsdp'}, dimensions={0}, use_global_device_ids=true | all-gather | bytes 959616 | tf_op jit(solution)/shard_map/all_gather | solution.py:873
  41.9 16.7 %collective-permute-done.7.refs_1_ = bf16[128,1088]{1,0:T(8,128)(2,1)S(1)} collective-permute-done((bf16[128,1088]{1,0:T(8,128)(2,1)}, bf16[128,1088]{1,0:T(8,128)(2,1)S(1)}, u32[]{:S(2)}, u32[]{:S(2)}) %collective-permute-start.7) | collective-permute-done | bytes 278560 | tf_op jit(solution)/shard_map/ppermute | solution.py:51
  61.3 5.8 %collective-permute-start.2 = (bf16[136,1088]{1,0:T(8,128)(2,1)S(1)}, bf16[136,1088]{1,0:T(8,128)(2,1)S(1)}, u32[]{:S(2)}, u32[]{:S(2)}) collective-permute-start(bf16[136,1088]{1,0:T(8,128)(2,1)S(1)} %copy-done.9), channel_id=1, source_target_pairs={{6,0},{7,1},{0,2},{1,3},{2,4},{3,5},{4,6},{5,7},{14,8},{15,9},{8,1... | collective-permute-start | bytes 887816 | tf_op jit(solution)/shard_map/ppermute | solution.py:51
  73.2 6.2 %collective-permute-done.2.refs_3_.refs_11_ = bf16[136,1088]{1,0:T(8,128)(2,1)S(1)} collective-permute-done((bf16[136,1088]{1,0:T(8,128)(2,1)S(1)}, bf16[136,1088]{1,0:T(8,128)(2,1)S(1)}, u32[]{:S(2)}, u32[]{:S(2)}) %collective-permute-start.2) | collective-permute-done | bytes 295968 | tf_op jit(solution)/shard_map/ppermute | solution.py:51
  93.0 12.8 %attention_forward.1 = (bf16[16,64,128]{2,1,0:T(8,128)(2,1)}, bf16[64,128]{1,0:T(8,128)(2,1)}, bf16[2048,64]{1,0:T(8,128)(2,1)}, bf16[2048,64]{1,0:T(8,128)(2,1)...) custom-call(s32[32]{0:T(128)} %table_ref.3, ...), custom_call_target="tpu_custom_call" | custom-call | flops 8000000000 | bytes 7482880 | tf_op jit(solution)/shard_map/attention_forward/pallas_call | solution.py:110
  105.8 8.3 %all-to-all-start = ((bf16[16,64,128]{2,1,0:T(8,128)(2,1)}), bf16[16,64,128]{2,1,0:T(8,128)(2,1)S(1)}, u32[]{:S(2)}, u32[]{:S(2)}) async-start(bf16[16,64,128]{2,1,0:T(8,128)(2,1)} %get-tuple-element.84), calls=%async_computation | async-start | bytes 524288 | tf_op jit(solution)/shard_map/all_to_all | solution.py:934
  115.1 7.9 %all-to-all-done.recv_ref = bf16[16,64,128]{2,1,0:T(8,128)(2,1)S(1)} async-done(((bf16[16,64,128]{2,1,0:T(8,128)(2,1)}), bf16[16,64,128]{2,1,0:T(8,128)(2,1)S(1)}, u32[]{:S(2)}, u32[]{:S(2)}) %all-to-all-start) | async-done | bytes 262176 | tf_op jit(solution)/shard_map/all_to_all | solution.py:934
  130.1 27.4 %all-gather.8.cloned.1.call-done.values_ref = bf16[1024,1088]{1,0:T(8,128)(2,1)} async-done(((bf16[128,1088]{1,0:T(8,128)(2,1)}), bf16[1024,1088]{1,0:T(8,128)(2,1)}) %all-gather.8.cloned.1.call-update) | async-done | bytes 2228240 | tf_op jit(solution)/shard_map/all_gather | solution.py:938
  157.5 11.5 %hidden_pass.1 = (bf16[1024,544]{1,0:T(8,128)(2,1)}, bf16[1024,544]{1,0:T(8,128)(2,1)}, f32[4,128,1152]{2,1,0:T(8,128)}, bf16[4,128,1152]{2,1,0:T(8,128)(2,1)}) custom-call(s32[2]{0:T(128)} %pad_add_fusion.1.at_ref, bf16[1024,1088]{1,0:T(8,128)(2,1)} %all-gather.8.cloned.1.call-done.values_ref, bf16[128,1088]{1,0:T(8,128)(2,1)} %bitcast.14.refs_0_.refs_4_.grad_ref, ...), custom_call_target="tpu_custom_call" | custom-call | flops 3636461568 | bytes 12601984 | tf_op jit(solution)/shard_map/hidden_pass/pallas_call | solution.py:110
  181.5 10.0 %hidden_grads.1 = (f32[4,128,1152]{2,1,0:T(8,128)}, bf16[4,128,1152]{2,1,0:T(8,128)(2,1)}, bf16[544,1088]{1,0:T(8,128)(2,1)}, bf16[8,144,544]{2,1,0:T(8,128)(2,1)}) custom-call(s32[2]{0:T(128)} %pad_add_fusion.1.at_ref, bf16[1024,1088]{1,0:T(8,128)(2,1)} %all-gather.8.cloned.1.call-done.values_ref, bf16[128,1088]{1,0:T(8,128)(2,1)} %bitcast.14.refs_0_.refs_4_.grad_ref, ...), custom_call_target="tpu_custom_call" | custom-call | flops 3636461568 | bytes 13844480 | tf_op jit(solution)/shard_map/hidden_grads/pallas_call | solution.py:110
  194.5 4.4 %mixed_grads.1 = (f32[128,1088]{1,0:T(8,128)}, bf16[128,1088]{1,0:T(8,128)(2,1)}, bf16[16,64,128]{2,1,0:T(8,128)(2,1)}, bf16[64,128]{1,0:T(8,128)(2,1)}) custom-call(s32[2]{0:T(128)} %pad_add_fusion.1.at_ref, f32[128,1152]{1,0:T(8,128)} %get-tuple-element.100.refs_0_, bf16[128,1152]{1,0:T(8,128)(2,1)} %copy-done.24, bf16[128,1152]{1,0:T(8,128)(2,1)} %copy-done.25, ...), custom_call_target="tpu_custom_call" | custom-call | flops 303038464 | bytes 5796608 | tf_op jit(solution)/shard_map/mixed_grads/pallas_call | solution.py:110
  203.5 7.0 %all-to-all-start.2 = ((bf16[16,64,128]{2,1,0:T(8,128)(2,1)}), bf16[16,64,128]{2,1,0:T(8,128)(2,1)S(1)}, u32[]{:S(2)}, u32[]{:S(2)}) async-start(bf16[16,64,128]{2,1,0:T(8,128)(2,1)} %get-tuple-element.115), calls=%async_computation.2 | async-start | bytes 524288 | tf_op jit(solution)/shard_map/all_to_all | solution.py:967
  224.8 13.2 %attention_backward.1 = (bf16[16,320,128]{2,1,0:T(8,128)(2,1)}, bf16[64,128]{1,0:T(8,128)(2,1)}, bf16[2048,384]{1,0:T(8,128)(2,1)}) custom-call(s32[32]{0:T(128)} %table_ref.3, s32[1]{0:T(128)} %bitcast.2.at_ref, bf16[16,64,128]{2,1,0:T(8,128)(2,1)} %copy-done.28, bf16[64,128]{1,0:T(8,128)(2,1)} %get-tuple-element.121.grad_last_ref, ...), custom_call_target="tpu_custom_call" | custom-call | flops 12000000000 | bytes 5080576 | tf_op jit(solution)/shard_map/attention_backward/pallas_call | solution.py:110
  238.1 6.7 %projection_grads.1 = (f32[4,144,384]{2,1,0:T(8,128)}, bf16[4,144,384]{2,1,0:T(8,128)(2,1)}) custom-call(s32[2]{0:T(128)} %pad_add_fusion.1.at_ref, bf16[2048,1088]{1,0:T(8,128)(2,1)} %all-gather.4.cloned.1.call-done.scaled_ref, bf16[2048,384]{1,0:T(8,128)(2,1)} %get-tuple-element.134.grads_ref), custom_call_target="tpu_custom_call" | custom-call | flops 1711276032 | bytes 7356416 | tf_op jit(solution)/shard_map/projection_grads/pallas_call | solution.py:110
  258.0 7.0 %collective-permute-done.30 = bf16[144,1152]{1,0:T(8,128)(2,1)S(1)} collective-permute-done((bf16[144,1152]{1,0:T(8,128)(2,1)S(1)}, bf16[144,1152]{1,0:T(8,128)(2,1)S(1)}, u32[]{:S(2)}, u32[]{:S(2)}) %collective-permute-start.30) | collective-permute-done | bytes 331808 | tf_op jit(solution)/shard_map/ppermute | solution.py:51
  279.1 8.3 %all-to-all-start.3 = ((bf16[16,320,128]{2,1,0:T(8,128)(2,1)}), bf16[16,320,128]{2,1,0:T(8,128)(2,1)S(1)}, u32[]{:S(2)}, u32[]{:S(2)}) async-start(bf16[16,320,128]{2,1,0:T(8,128)(2,1)} %get-tuple-element.132), calls=%async_computation.3 | async-start | bytes 2621440 | tf_op jit(solution)/shard_map/all_to_all | solution.py:983
  288.5 8.5 %collective-permute-done.33 = bf16[144,1152]{1,0:T(8,128)(2,1)S(1)} collective-permute-done((bf16[144,1152]{1,0:T(8,128)(2,1)S(1)}, bf16[144,1152]{1,0:T(8,128)(2,1)S(1)}, u32[]{:S(2)}, u32[]{:S(2)}) %collective-permute-start.33) | collective-permute-done | bytes 331808 | tf_op jit(solution)/shard_map/ppermute | solution.py:51
  297.2 26.2 %all-reduce.3.cloned.1.call-done = (bf16[544,1088]{1,0:T(8,128)(2,1)}, bf16[8,144,544]{2,1,0:T(8,128)(2,1)}) async-done(((bf16[544,1088]{1,0:T(8,128)(2,1)}, bf16[8,144,544]{2,1,0:T(8,128)(2,1)}), (bf16[544,1088]{1,0:T(8,128)(2,1)}, bf16[8,144,544]{2,1,0:T(8,128)(2,1)})) %all-reduce.3.cloned.1.call-update) | async-done | bytes 2437136 | tf_op jit(solution)/shard_map/psum | solution.py:955
  336.4 12.7 %all-to-all-done.5.moment_ref = bf16[8,144,544]{2,1,0:T(8,128)(2,1)S(1)} async-done(((bf16[8,144,544]{2,1,0:T(8,128)(2,1)}), bf16[8,144,544]{2,1,0:T(8,128)(2,1)S(1)}, u32[]{:S(2)}, u32[]{:S(2)}) %all-to-all-start.5) | async-done | bytes 1253408 | tf_op jit(solution)/shard_map/all_to_all | solution.py:1015
  350.8 5.2 %all-to-all-start.4 = ((bf16[16,144,384]{2,1,0:T(8,128)(2,1)}), bf16[16,144,384]{2,1,0:T(8,128)(2,1)S(1)}, u32[]{:S(2)}, u32[]{:S(2)}) async-start(bf16[16,144,384]{2,1,0:T(8,128)(2,1)} %broadcast_in_dim.92), calls=%async_computation.4 | async-start | bytes 3538944 | tf_op jit(solution)/shard_map/all_to_all | solution.py:988
  357.4 6.0 %fusion.9 = (f32[128]{0:T(128)S(1)}, f32[128]{0:T(128)S(1)}, f32[128,1088]{1,0:T(8,128)S(1)}) fusion(f32[128]{0:T(128)S(1)} %add_rsqrt_fusion, f32[128]{0:T(128)S(1)} %broadcast_multiply_fusion.2, bf16[1,128,1088]{2,1,0:T(8,128)(2,1)S(1)} %copy-done.1, f32[1088]{0:T(1024)S(1)} %get-tuple-element.212, bf16[3264,128]{1,0:T(8,128)(2,1)} %slice_dynamic-update-slice_fusion, ...), kind=kOutput, calls=%fused_computation.68 | convolution fusion | flops 910089984 | bytes 8780032 | tf_op jit(solution)/shard_map/dot_general | solution.py:24
  364.6 6.0 %finish_up.1 = (f32[136,4352]{1,0:T(8,128)}, f32[136,1]{1,0:T(8,128)}, f32[136,1]{1,0:T(8,128)}, f32[1,544]{1,0:T(1,128)}) custom-call(s32[1]{0:T(128)} %bitcast.22.at_ref, bf16[8,144,544]{2,1,0:T(8,128)(2,1)} %copy-done.3, bf16[136,4352]{1,0:T(8,128)(2,1)} %w_ref.3, f32[136,1]{1,0:T(8,128)} %copy.89.gain_ref, f32[136,1]{1,0:T(8,128)} %copy.90.shift_ref), custom_call_target="tpu_custom_call" | custom-call | bytes 4808960 | tf_op jit(solution)/shard_map/finish_up/pallas_call | solution.py:110
  373.8 8.0 %all-to-all-done.4.head_ref = bf16[16,144,384]{2,1,0:T(8,128)(2,1)S(1)} async-done(((bf16[16,144,384]{2,1,0:T(8,128)(2,1)}), bf16[16,144,384]{2,1,0:T(8,128)(2,1)S(1)}, u32[]{:S(2)}, u32[]{:S(2)}) %all-to-all-start.4) | async-done | bytes 1769504 | tf_op jit(solution)/shard_map/all_to_all | solution.py:988
  383.1 4.4 %finish_qkv.1 = (f32[136,3264]{1,0:T(8,128)}, f32[136,1]{1,0:T(8,128)}, f32[136,1]{1,0:T(8,128)}, f32[1,3264]{1,0:T(1,128)}) custom-call(bf16[16,144,384]{2,1,0:T(8,128)(2,1)} %copy-done.2, bf16[136,3264]{1,0:T(8,128)(2,1)} %w_ref.2, f32[136,1]{1,0:T(8,128)} %copy.87.gain_ref, f32[136,1]{1,0:T(8,128)} %copy.88.shift_ref), custom_call_target="tpu_custom_call" | custom-call | bytes 4448128 | tf_op jit(solution)/shard_map/finish_qkv/pallas_call | solution.py:110
  (264 shorter events, 138.6 us)
Async XLA Ops:
  7.2 76.2 %all-gather.4.cloned.1.call-start = ((), (), s32[]{:S(2)}) async-start(), calls=%async_computation.6 | async-start | bytes 5013504 | tf_op jit(solution)/shard_map/all_gather | solution.py:862
  29.8 53.6 %all-to-all-start.1 = ((bf16[8,136,544]{2,1,0:T(8,128)(2,1)}), bf16[8,136,544]{2,1,0:T(8,128)(2,1)S(1)}, u32[]{:S(2)}, u32[]{:S(2)}) async-start(bf16[8,136,544]{2,1,0:T(8,128)(2,1)} %bitcast.54), calls=%async_computation.1 | async-start | bytes 2785280 | tf_op jit(solution)/shard_map/all_to_all | solution.py:895
  33.6 95.9 %all-gather.6.cloned.1.call-start = ((), (), s32[]{:S(2)}) async-start(), calls=%async_computation.7 | async-start | bytes 8146944 | tf_op jit(solution)/shard_map/all_gather | solution.py:902
  34.6 24.0 %collective-permute-start.7 = (bf16[128,1088]{1,0:T(8,128)(2,1)}, bf16[128,1088]{1,0:T(8,128)(2,1)S(1)}, u32[]{:S(2)}, u32[]{:S(2)}) collective-permute-start(bf16[128,1088]{1,0:T(8,128)(2,1)} %bitcast.14.refs_0_.refs_4_.grad_ref), channel_id=1, source_target_pairs={{2,0},{3,1},{4,2},{5,3},{6,4},{7,5},{0,6},{1,7},{10,8},{11,9},{12,... | collective-permute-start | bytes 835592 | tf_op jit(solution)/shard_map/ppermute | solution.py:51
  37.8 23.5 %collective-permute-start.8 = (bf16[128,1088]{1,0:T(8,128)(2,1)}, bf16[128,1088]{1,0:T(8,128)(2,1)S(1)}, u32[]{:S(2)}, u32[]{:S(2)}) collective-permute-start(bf16[128,1088]{1,0:T(8,128)(2,1)} %bitcast.14.refs_0_.refs_4_.grad_ref), channel_id=1, source_target_pairs={{4,0},{5,1},{6,2},{7,3},{0,4},{1,5},{2,6},{3,7},{12,8},{13,9},{14,... | collective-permute-start | bytes 835592 | tf_op jit(solution)/shard_map/ppermute | solution.py:51
  38.6 28.4 %collective-permute-start.9 = (bf16[128,1088]{1,0:T(8,128)(2,1)}, bf16[128,1088]{1,0:T(8,128)(2,1)S(1)}, u32[]{:S(2)}, u32[]{:S(2)}) collective-permute-start(bf16[128,1088]{1,0:T(8,128)(2,1)} %bitcast.14.refs_0_.refs_4_.grad_ref), channel_id=1, source_target_pairs={{6,0},{7,1},{0,2},{1,3},{2,4},{3,5},{4,6},{5,7},{14,8},{15,9},{8,1... | collective-permute-start | bytes 835592 | tf_op jit(solution)/shard_map/ppermute | solution.py:51
  39.5 27.6 %collective-permute-start.10 = (bf16[128,1088]{1,0:T(8,128)(2,1)}, bf16[128,1088]{1,0:T(8,128)(2,1)S(1)}, u32[]{:S(2)}, u32[]{:S(2)}) collective-permute-start(bf16[128,1088]{1,0:T(8,128)(2,1)} %bitcast.14.refs_0_.refs_4_.grad_ref), channel_id=1, source_target_pairs={{1,0},{0,1},{3,2},{2,3},{5,4},{4,5},{7,6},{6,7},{9,8},{8,9},{11,10... | collective-permute-start | bytes 835592 | tf_op jit(solution)/shard_map/ppermute | solution.py:51
  39.5 32.2 %collective-permute-start = (bf16[136,1088]{1,0:T(8,128)(2,1)S(1)}, bf16[136,1088]{1,0:T(8,128)(2,1)S(1)}, u32[]{:S(2)}, u32[]{:S(2)}) collective-permute-start(bf16[136,1088]{1,0:T(8,128)(2,1)S(1)} %copy-done.9), channel_id=1, source_target_pairs={{2,0},{3,1},{4,2},{5,3},{6,4},{7,5},{0,6},{1,7},{10,8},{11,9},{12,... | collective-permute-start | bytes 887816 | tf_op jit(solution)/shard_map/ppermute | solution.py:51
  114.1 43.4 %all-gather.8.cloned.1.call-start = ((), (), s32[]{:S(2)}) async-start(), calls=%async_computation.8 | async-start | bytes 2654208 | tf_op jit(solution)/shard_map/all_gather | solution.py:938
  210.5 112.9 %all-reduce.3.cloned.1.call-start = ((), (), s32[]{:S(2)}) async-start(), calls=%async_computation.9 | async-start | bytes 5455872 | tf_op jit(solution)/shard_map/psum | solution.py:955
  219.8 25.0 %collective-permute-start.27 = (bf16[144,1152]{1,0:T(8,128)(2,1)}, bf16[144,1152]{1,0:T(8,128)(2,1)S(1)}, u32[]{:S(2)}, u32[]{:S(2)}) collective-permute-start(bf16[144,1152]{1,0:T(8,128)(2,1)} %get-tuple-element.143), channel_id=1, source_target_pairs={{6,0},{7,1},{0,2},{1,3},{2,4},{3,5},{4,6},{5,7},{14,8},{15,9},{8,1... | collective-permute-start | bytes 995336 | tf_op jit(solution)/shard_map/ppermute | solution.py:51
  221.4 23.3 %collective-permute-start.28 = (bf16[144,1152]{1,0:T(8,128)(2,1)}, bf16[144,1152]{1,0:T(8,128)(2,1)S(1)}, u32[]{:S(2)}, u32[]{:S(2)}) collective-permute-start(bf16[144,1152]{1,0:T(8,128)(2,1)} %get-tuple-element.144), channel_id=1, source_target_pairs={{4,0},{5,1},{6,2},{7,3},{0,4},{1,5},{2,6},{3,7},{12,8},{13,9},{14,... | collective-permute-start | bytes 995336 | tf_op jit(solution)/shard_map/ppermute | solution.py:51
  223.9 20.8 %collective-permute-start.29 = (bf16[144,1152]{1,0:T(8,128)(2,1)}, bf16[144,1152]{1,0:T(8,128)(2,1)S(1)}, u32[]{:S(2)}, u32[]{:S(2)}) collective-permute-start(bf16[144,1152]{1,0:T(8,128)(2,1)} %get-tuple-element.145), channel_id=1, source_target_pairs={{2,0},{3,1},{4,2},{5,3},{6,4},{7,5},{0,6},{1,7},{10,8},{11,9},{12,... | collective-permute-start | bytes 995336 | tf_op jit(solution)/shard_map/ppermute | solution.py:51
  244.9 20.0 %collective-permute-start.30 = (bf16[144,1152]{1,0:T(8,128)(2,1)S(1)}, bf16[144,1152]{1,0:T(8,128)(2,1)S(1)}, u32[]{:S(2)}, u32[]{:S(2)}) collective-permute-start(bf16[144,1152]{1,0:T(8,128)(2,1)S(1)} %add_convert_fusion.2), channel_id=1, source_target_pairs={{8,0},{16,8},{24,16},{0,24},{40,32},{48,40},{56,48},{32,56},{72,64... | collective-permute-start | bytes 995336 | tf_op jit(solution)/shard_map/ppermute | solution.py:51
  248.2 18.4 %collective-permute-start.31 = (bf16[144,1152]{1,0:T(8,128)(2,1)S(1)}, bf16[144,1152]{1,0:T(8,128)(2,1)S(1)}, u32[]{:S(2)}, u32[]{:S(2)}) collective-permute-start(bf16[144,1152]{1,0:T(8,128)(2,1)S(1)} %add_convert_fusion.2), channel_id=1, source_target_pairs={{16,0},{24,8},{0,16},{8,24},{48,32},{56,40},{32,48},{40,56},{80,64... | collective-permute-start | bytes 995336 | tf_op jit(solution)/shard_map/ppermute | solution.py:51
  249.3 19.9 %collective-permute-start.32 = (bf16[144,1152]{1,0:T(8,128)(2,1)S(1)}, bf16[144,1152]{1,0:T(8,128)(2,1)S(1)}, u32[]{:S(2)}, u32[]{:S(2)}) collective-permute-start(bf16[144,1152]{1,0:T(8,128)(2,1)S(1)} %add_convert_fusion.2), channel_id=1, source_target_pairs={{24,0},{0,8},{8,16},{16,24},{56,32},{32,40},{40,48},{48,56},{88,64... | collective-permute-start | bytes 995336 | tf_op jit(solution)/shard_map/ppermute | solution.py:51
  254.4 19.2 %collective-permute-start.20 = (bf16[128,1152]{1,0:T(8,128)(2,1)}, bf16[128,1152]{1,0:T(8,128)(2,1)S(1)}, u32[]{:S(2)}, u32[]{:S(2)}) collective-permute-start(bf16[128,1152]{1,0:T(8,128)(2,1)} %get-tuple-element.112), channel_id=1, source_target_pairs={{4,0},{5,1},{6,2},{7,3},{0,4},{1,5},{2,6},{3,7},{12,8},{13,9},{14,... | collective-permute-start | bytes 884744 | tf_op jit(solution)/shard_map/ppermute | solution.py:51
  269.2 18.2 %collective-permute-start.25 = (bf16[144,384]{1,0:T(8,128)(2,1)}, bf16[144,384]{1,0:T(8,128)(2,1)}, u32[]{:S(2)}, u32[]{:S(2)}) collective-permute-start(bf16[144,384]{1,0:T(8,128)(2,1)} %get-tuple-element.139), channel_id=1, source_target_pairs={{4,0},{5,1},{6,2},{7,3},{0,4},{1,5},{2,6},{3,7},{12,8},{13,9},{14,... | collective-permute-start | bytes 331784 | tf_op jit(solution)/shard_map/ppermute | solution.py:51
  273.6 23.4 %collective-permute-start.33 = (bf16[144,1152]{1,0:T(8,128)(2,1)S(1)}, bf16[144,1152]{1,0:T(8,128)(2,1)S(1)}, u32[]{:S(2)}, u32[]{:S(2)}) collective-permute-start(bf16[144,1152]{1,0:T(8,128)(2,1)S(1)} %add_convert_fusion.1), channel_id=1, source_target_pairs={{32,0},{40,8},{48,16},{56,24},{64,32},{72,40},{80,48},{88,56},{96,... | collective-permute-start | bytes 995336 | tf_op jit(solution)/shard_map/ppermute | solution.py:51
  276.3 20.7 %collective-permute-start.34 = (bf16[144,1152]{1,0:T(8,128)(2,1)S(1)}, bf16[144,1152]{1,0:T(8,128)(2,1)S(1)}, u32[]{:S(2)}, u32[]{:S(2)}) collective-permute-start(bf16[144,1152]{1,0:T(8,128)(2,1)S(1)} %add_convert_fusion.1), channel_id=1, source_target_pairs={{64,0},{72,8},{80,16},{88,24},{96,32},{104,40},{112,48},{120,56},{... | collective-permute-start | bytes 995336 | tf_op jit(solution)/shard_map/ppermute | solution.py:51
  277.0 20.0 %collective-permute-start.35 = (bf16[144,1152]{1,0:T(8,128)(2,1)S(1)}, bf16[144,1152]{1,0:T(8,128)(2,1)S(1)}, u32[]{:S(2)}, u32[]{:S(2)}) collective-permute-start(bf16[144,1152]{1,0:T(8,128)(2,1)S(1)} %add_convert_fusion.1), channel_id=1, source_target_pairs={{96,0},{104,8},{112,16},{120,24},{0,32},{8,40},{16,48},{24,56},{32... | collective-permute-start | bytes 995336 | tf_op jit(solution)/shard_map/ppermute | solution.py:51
  279.1 45.2 %all-to-all-start.3 = ((bf16[16,320,128]{2,1,0:T(8,128)(2,1)}), bf16[16,320,128]{2,1,0:T(8,128)(2,1)S(1)}, u32[]{:S(2)}, u32[]{:S(2)}) async-start(bf16[16,320,128]{2,1,0:T(8,128)(2,1)} %get-tuple-element.132), calls=%async_computation.3 | async-start | bytes 2621440 | tf_op jit(solution)/shard_map/all_to_all | solution.py:983
  324.3 24.8 %all-to-all-start.5 = ((bf16[8,144,544]{2,1,0:T(8,128)(2,1)}), bf16[8,144,544]{2,1,0:T(8,128)(2,1)S(1)}, u32[]{:S(2)}, u32[]{:S(2)}) async-start(bf16[8,144,544]{2,1,0:T(8,128)(2,1)} %get-tuple-element.146), calls=%async_computation.5 | async-start | bytes 2949120 | tf_op jit(solution)/shard_map/all_to_all | solution.py:1015
  350.8 31.0 %all-to-all-start.4 = ((bf16[16,144,384]{2,1,0:T(8,128)(2,1)}), bf16[16,144,384]{2,1,0:T(8,128)(2,1)S(1)}, u32[]{:S(2)}, u32[]{:S(2)}) async-start(bf16[16,144,384]{2,1,0:T(8,128)(2,1)} %broadcast_in_dim.92), calls=%async_computation.4 | async-start | bytes 3538944 | tf_op jit(solution)/shard_map/all_to_all | solution.py:988
  (71 other events, 635.4 us)
Sparse Core Ops, SparseCore 0:
  10.8 56.5 all-gather.3
  83.6 45.8 all-gather.5
  131.8 25.7 all-gather.7
  215.1 108.2 all-reduce.2
